TPU v7x, 128 devices: a whole 4x4x4 slice. The times are simulated.
128 devices in a mesh: row: 16 (over y_lo, x, core), col: 8 (over y_hi, z).
Axes of the slice: x: 4, y: 4 (y_hi: 2, y_lo: 2; y = y_hi * 2 + y_lo), z: 4, core: 2. Of those that a mesh axis runs over, the one named last changes fastest.
Arguments:
- eigvecs: float32 [8, 256, 131072], P('col', 'row'), may hold values from -6 to 6
- reflectors: float32 [8, 131072, 256], P('col', 'row'), may hold values from -6 to 6
- factors: float32 [8, 256, 256], P('col'), may hold values from -7.6293945e-06 to 3.0517578e-05, as said below
- owner: int32 [8], replicated, may hold values from 0 to 7, each once
Outputs:
- back_vectors: float32 [8, 256, 131072], P('col', None, 'row')
Inputs may be any that keep to these rules, and one draw needn't show every extreme that they name: Each factors[c] is upper triangular with a positive diagonal.
All inputs are finite; a program needn't handle non-finite values.
Results may differ from a plain program's by a relative error of at most 0.0001.
Values sent between devices are 32-bit elements; how exact they have to be, the bound alone decides.
No kernel may reach another device: no remote copies, remote signals or barrier semaphores. Data moves between devices by JAX's collectives and lax.ppermute only.
A program may use at most 192 MiB of HBM per device.

v0:
```python
import functools

import jax
import jax.numpy as jnp
from jax import lax
from jax.experimental import pallas as pl
from jax.experimental.pallas import tpu as pltpu
from jax.sharding import PartitionSpec as P

RING = 4
GROUPS = 2
QUARTER = 3
CHUNKS = RING * QUARTER
SLOTS = max(CHUNKS + 2, 3 * QUARTER + 5)
STEPS = (1, -1)
BLOCKS = (1, 0)
MOVES = ((0, 1), (10, 0))
TILE = 512
VMEM = 48 * 2**20
GRANT = 50 * 2**20
F32 = jnp.float32
ANY = pl.BlockSpec(memory_space=pl.ANY)
HBM = pl.BlockSpec(memory_space=pltpu.HBM)
SMEM = pl.BlockSpec(memory_space=pltpu.SMEM)


def ring_pairs(step):
    return [(h * RING + z, h * RING + (z + step) % RING) for h in range(2) for z in range(RING)]


SWAP = [(i, (i + RING) % (2 * RING)) for i in range(2 * RING)]


def chunk_rows(part):
    return -(-part // (CHUNKS * 8)) * 8


def crossing_id(batch, place):
    return jnp.where(place == 0, 3 * QUARTER + batch, 3 * batch + 3 - place)


def cross_slots(s):
    send = next((b for b in range(QUARTER) if s == 3 * b + 3), None)
    inject = next((b for b in range(QUARTER) if s == 3 * b + 5), None)
    return send, inject


def plan(s, owner, step):
    me = lax.axis_index("col")
    far = me // RING != owner // RING
    place = jnp.bitwise_and(step * (me - owner), RING - 1)
    source = me == owner
    _, inject = cross_slots(s)
    index = s - place
    keep = (index >= 0) & (index < CHUNKS) & ~far
    if s == 0:
        keep = source
    for b in range(QUARTER):
        j = s - 1 - (3 * b + 5)
        if 0 <= j < 3:
            index = jnp.where(far, crossing_id(b, jnp.bitwise_and(place - 1 - j, RING - 1)), index)
            keep = keep | far
    index = jnp.clip(index, 0, CHUNKS - 1)
    cross = crossing_id(inject, place) if inject is not None else 0
    return source, index, keep, far, cross


def slot_body(s, group, n_deps, owner_ref, own_ref, *refs):
    refs = list(refs)
    over, inject = cross_slots(s)
    first = s == 0 and group == 0
    none = [None, None]
    heads = [refs.pop(0), refs.pop(0)] if group == 0 else none
    got = [refs.pop(0), refs.pop(0)] if s else none
    crossed = [refs.pop(0), refs.pop(0)] if inject is not None else none
    del refs[: n_deps + (0 if first else 2)]
    held = [refs.pop(0), refs.pop(0)]
    send = [refs.pop(0), refs.pop(0)] if s < SLOTS else none
    across = [refs.pop(0), refs.pop(0)] if over is not None else none
    sems = refs.pop(0)
    part = own_ref.shape[1] // GROUPS
    size = chunk_rows(part)

    now, then = [], []
    for i in range(2):
        source, index, keep, far, cross = plan(s, owner_ref[BLOCKS[i]], STEPS[i])

        def own(c):
            start = min(c * size, part - size)
            if group == 0 and start + size <= heads[i].shape[0]:
                return heads[i].at[pl.ds(start, size)]
            return own_ref.at[0, pl.ds(group * part + start, size)]

        def slot(index):
            start = group * part + jnp.minimum(index * size, part - size)
            return held[i].at[pl.ds(pl.multiple_of(start, 8), size)]

        if s == 0:
            now.append((True, own(0), send[i]))
        elif s < CHUNKS:
            now.append((source, own(s), send[i]))
        passes = ~source if 0 < s < CHUNKS else True
        if inject is not None:
            now.append((far, crossed[i], send[i]))
            now.append((far, crossed[i], slot(cross)))
            passes = ~far if passes is True else passes & ~far
        if 0 < s < SLOTS:
            now.append((passes, got[i], send[i]))
        if s < CHUNKS:
            then.append((source, send[i], slot(s)))
        if s:
            now.append((keep & ~source, got[i], slot(index)))
        if over is not None:
            now.append((source, own(3 * QUARTER + over), across[i]))
            now.append((~source, got[i], across[i]))

    for copies in (now, then):
        for wait in (False, True):
            for n, (when, src, dst) in enumerate(copies):
                copy = pltpu.make_async_copy(src, dst, sems.at[n])
                act = copy.wait if wait else copy.start
                act() if when is True else pl.when(when)(act)


def slot_call(s, group, owner, own, heads, got, crossed, held, deps):
    part, width = own.shape[1] // GROUPS, own.shape[2]
    size = chunk_rows(part)
    chunk = jax.ShapeDtypeStruct((size, width), own.dtype)
    over, inject = cross_slots(s)
    ins, specs = [owner, own], [SMEM, HBM]

    def add(arrays, spec):
        ins.extend(arrays)
        specs.extend([spec] * len(arrays))

    if group == 0:
        add(heads, ANY)
    if s:
        add(got, ANY)
    if inject is not None:
        add(crossed, ANY)
    add(deps, ANY)
    first = len(ins)
    if held is not None:
        add(held, HBM)
    outs = [jax.ShapeDtypeStruct(own.shape[1:], own.dtype)] * 2
    if s < SLOTS:
        outs += [chunk] * 2
    if over is not None:
        outs += [chunk] * 2
    out = pl.pallas_call(
        functools.partial(slot_body, s, group, len(deps)),
        out_shape=outs,
        in_specs=specs,
        out_specs=[HBM] * 2 + [ANY] * (len(outs) - 2),
        scratch_shapes=[pltpu.SemaphoreType.DMA((16,))],
        input_output_aliases={} if held is None else {first: 0, first + 1: 1},
        compiler_params=pltpu.CompilerParams(vmem_limit_bytes=GRANT),
        cost_estimate=pl.CostEstimate(flops=0, bytes_accessed=4 * 2**20, transcendentals=0),
        name=f"slot{s}_{group}",
    )(*ins)
    held, out = out[:2], out[2:]
    send = across = None
    if s < SLOTS:
        send, out = out[:2], out[2:]
    if over is not None:
        across = out
    return held, send, across


def regroup_body(first, groups, x_ref, dep_ref, out_ref, room, sems):
    rows = out_ref.shape[2]

    def come(j):
        src = x_ref.at[0, pl.ds(first, out_ref.shape[1]), pl.ds(j * rows, rows)]
        return pltpu.make_async_copy(src, room.at[j], sems.at[0, j])

    def leave(j):
        return pltpu.make_async_copy(room.at[j], out_ref.at[j], sems.at[1, j])

    for j in range(groups):
        come(j).start()
    for j in range(groups):
        come(j).wait()
        leave(j).start()
    for j in range(groups):
        leave(j).wait()


def regroup(x, first, count, groups, dep):
    shape = (groups, count, x.shape[2] // groups)
    return pl.pallas_call(
        functools.partial(regroup_body, first, groups),
        out_shape=jax.ShapeDtypeStruct(shape, x.dtype),
        in_specs=[HBM, ANY],
        out_specs=HBM,
        scratch_shapes=[pltpu.VMEM(shape, x.dtype), pltpu.SemaphoreType.DMA((2, groups))],
        compiler_params=pltpu.CompilerParams(vmem_limit_bytes=GRANT),
        name="regroup",
    )(x, dep)


def parts_of(x):
    high = x.astype(jnp.bfloat16)
    low = (x - high.astype(F32)).astype(jnp.bfloat16)
    return high, low


def dot3(left, right, dims):
    (lh, ll), (rh, rl) = left, right
    go = functools.partial(lax.dot_general, dimension_numbers=(dims, ((), ())), preferred_element_type=F32)
    return go(lh, rh) + (go(lh, rl) + go(ll, rh))


def full(left, right, dims):
    return lax.dot_general(
        left, right, (dims, ((), ())), precision=lax.Precision.HIGHEST, preferred_element_type=F32
    )


def project_body(xa_ref, xb_ref, p1_ref, p0_ref, out_ref):
    half = xa_ref.shape[0]
    p1, p0 = parts_of(p1_ref[...]), parts_of(p0_ref[...])

    @pl.when(pl.program_id(0) == 0)
    def _():
        out_ref[...] = jnp.zeros_like(out_ref)

    for t, ref in enumerate((xa_ref, xb_ref)):
        x = parts_of(ref[...])
        at = pl.ds(t * half, half)
        out_ref[0, at] += dot3(x, p1, ((1,), (0,)))
        out_ref[1, at] += dot3(x, p0, ((1,), (0,)))
    out_ref[2] += dot3(p1, p0, ((0,), (0,)))


def project(fields, held):
    rows, width = held[0].shape
    xspec = pl.BlockSpec((fields[0].shape[0], TILE), lambda i: (0, i))
    pspec = pl.BlockSpec((TILE, width), lambda i: (i, 0))
    return pl.pallas_call(
        project_body,
        out_shape=jax.ShapeDtypeStruct((3, width, width), F32),
        grid=(rows // TILE,),
        in_specs=[xspec, xspec, pspec, pspec],
        out_specs=pl.BlockSpec((3, width, width), lambda i: (0, 0, 0)),
        compiler_params=pltpu.CompilerParams(vmem_limit_bytes=VMEM),
        name="project",
    )(*fields, *held)


def update_body(sum_ref, f1_ref, f0_ref, xa_ref, xb_ref, p1_ref, p0_ref, out_ref, y_ref):
    @pl.when(pl.program_id(0) == 0)
    def _():
        y1 = full(sum_ref[0], f1_ref[...], ((1,), (1,)))
        w0 = sum_ref[1] - full(y1, sum_ref[2], ((1,), (0,)))
        y0 = full(w0, f0_ref[...], ((1,), (1,)))
        for i, y in enumerate((y1, y0)):
            high, low = parts_of(y)
            y_ref[i, 0] = high
            y_ref[i, 1] = low

    change = 0
    for i, ref in enumerate((p1_ref, p0_ref)):
        change += dot3((y_ref[i, 0], y_ref[i, 1]), parts_of(ref[...]), ((1,), (1,)))
    n, _, sub, rows = out_ref.shape
    for t, ref in enumerate((xa_ref, xb_ref)):
        half = ref.shape[0]
        out_ref[:, t] = (ref[...] - change[t * half : (t + 1) * half]).reshape(n, sub, rows)


def update(total, factors, fields, held, groups):
    rows, width = held[0].shape
    half = fields[0].shape[0]
    xspec = pl.BlockSpec((half, TILE), lambda i: (0, i))
    pspec = pl.BlockSpec((TILE, width), lambda i: (i, 0))
    whole = pl.BlockSpec(memory_space=pltpu.VMEM)
    return pl.pallas_call(
        update_body,
        out_shape=jax.ShapeDtypeStruct((groups, 2, half // groups, rows), F32),
        grid=(rows // TILE,),
        in_specs=[whole, whole, whole, xspec, xspec, pspec, pspec],
        out_specs=pl.BlockSpec((groups, 2, half // groups, TILE), lambda i: (0, 0, 0, i)),
        scratch_shapes=[pltpu.VMEM((2, 2, width, width), jnp.bfloat16)],
        compiler_params=pltpu.CompilerParams(vmem_limit_bytes=VMEM),
        name="update",
    )(total, *factors, *fields, *held)


def shared_factors(factor, owner):
    second = lax.axis_index("row") % 2 == 1
    mine = jnp.where(lax.axis_index("col") == jnp.where(second, owner[0], owner[1]), factor, 0.0)
    for pairs in (ring_pairs(1), ring_pairs(2), SWAP):
        mine = mine + lax.ppermute(mine, "col", pairs)
    other = lax.ppermute(mine, "row", [(i, i ^ 1) for i in range(lax.axis_size("row"))])
    return [jnp.where(second, other, mine), jnp.where(second, mine, other)]


def shards(eigvecs, reflectors, factors, owner):
    groups = lax.axis_size("row")
    own_count = eigvecs.shape[1]
    rows_here = eigvecs.shape[2] // groups
    width = factors.shape[2]
    used = shared_factors(factors[0], owner)

    size = chunk_rows(rows_here // GROUPS)
    top = -(-2 * width // size) * size
    heads = []
    for block in BLOCKS:
        rows = lax.axis_index("row") * rows_here + lax.broadcasted_iota(jnp.int32, (top, width), 0)
        cols = lax.broadcasted_iota(jnp.int32, (top, width), 1) + block * width
        head = jnp.where(rows > cols, reflectors[0, :top], 0.0)
        heads.append(jnp.where(rows == cols, 1.0, head))
    held = None
    got = [None] * GROUPS
    crossed = [None] * GROUPS
    turns = [ring_pairs(step) for step in STEPS]
    fields = []
    deps = {}
    for s in range(SLOTS + 1):
        for g in range(GROUPS):
            held, send, across = slot_call(
                s, g, owner, reflectors, heads, got[g], crossed[g], held, deps.get((s, g), [])
            )
            if send is not None:
                got[g] = [lax.ppermute(x, "col", turn) for x, turn in zip(send, turns)]
            if across is not None:
                crossed[g] = [lax.ppermute(x, "col", SWAP) for x in across]
            if (s, g) in MOVES:
                half = own_count // 2
                split = regroup(eigvecs, len(fields) * half, half, groups, send[0])
                moved = lax.all_to_all(split, "row", split_axis=0, concat_axis=0, tiled=True)
                fields.append(moved.reshape(groups * half, rows_here))
                if len(fields) == 1:
                    deps = {(1, 0): [split], (6, 0): [fields[0]], (11, 1): used}

    stack = project(fields, held).reshape(groups, 3 * width // groups, width)
    cut = jnp.sum(lax.all_to_all(stack, "row", split_axis=0, concat_axis=0, tiled=True), 0)
    total = lax.all_gather(cut, "row", axis=0, tiled=True).reshape(3, width, width)
    out = update(total, used, fields, held, groups)
    return out.reshape(1, own_count * groups, rows_here)


def solution(mesh):
    in_specs = (P("col", "row", None), P("col", "row", None), P("col", None, None), P())
    out_specs = P("col", None, "row")
    return jax.shard_map(shards, mesh=mesh, in_specs=in_specs, out_specs=out_specs, check_vma=False)
```

profile of v0, /device:TPU:1, one launch (start us, length us, event | category | flops | bytes accessed | tf_op | source)
XLA Modules:
  0.0 393.8 jit_solution(9523781299161059268)
XLA Ops:
  3.0 1.9 slot0_1.1
  4.9 3.9 regroup.2.refs_4_
  8.8 6.8 %all-to-all-start = ((f32[16,8,8192]{2,1,0:T(8,128)}), f32[16,8,8192]{2,1,0:T(8,128)}, u32[]{:S(2)}, u32[]{:S(2)}) async-start(f32[16,8,8192]{2,1,0:T(8,128)} %regroup.2.refs_4_), calls=%async_computation | async-start | bytes 8388608 | tf_op jit(solution)/shard_map/all_to_all | solution.py:332
  15.6 3.1 collective-permute-start
  20.2 2.0 collective-permute-start.5
  22.1 5.8 %collective-permute-done.refs_2_ = f32[344,256]{1,0:T(8,128)S(1)} collective-permute-done((f32[344,256]{1,0:T(8,128)S(1)}, f32[344,256]{1,0:T(8,128)S(1)}, u32[]{:S(2)}, u32[]{:S(2)}) %collective-permute-start) | collective-permute-done | bytes 352288 | tf_op jit(solution)/shard_map/ppermute | solution.py:326
  31.9 3.6 collective-permute-done.4.refs_0_
  39.4 3.6 collective-permute-done.2.refs_2_
  47.2 3.4 collective-permute-done.8.refs_0_
  54.8 3.4 collective-permute-done.6.refs_2_
  62.6 3.0 collective-permute-done.12.refs_0_
  70.1 3.8 collective-permute-start.16
  77.3 3.0 collective-permute-done.18.refs_0_
  80.3 2.9 collective-permute-start.24
  86.1 2.2 collective-permute-start.25
  88.2 2.7 collective-permute-start.23
  93.0 2.3 collective-permute-done.24.refs_2_
  95.5 7.4 %collective-permute-done.25.refs_3_ = f32[344,256]{1,0:T(8,128)S(1)} collective-permute-done((f32[344,256]{1,0:T(8,128)S(1)}, f32[344,256]{1,0:T(8,128)S(1)}, u32[]{:S(2)}, u32[]{:S(2)}) %collective-permute-start.25) | collective-permute-done | bytes 352288 | tf_op jit(solution)/shard_map/ppermute | solution.py:328
  104.7 2.7 collective-permute-start.29
  107.3 1.9 slot6_0.1
  109.3 2.7 collective-permute-start.27
  115.5 2.6 collective-permute-start.35
  118.1 4.2 %collective-permute-start.32 = (f32[344,256]{1,0:T(8,128)S(1)}, f32[344,256]{1,0:T(8,128)S(1)}, u32[]{:S(2)}, u32[]{:S(2)}) collective-permute-start(f32[344,256]{1,0:T(8,128)S(1)} %get-tuple-element.193), channel_id=1, source_target_pairs={{0,4},{1,5},{2,6},{3,7},{4,0},{5,1},{6,2},{7,3},{8,12},{9,13},{10,... | collective-permute-start | bytes 1056776 | tf_op jit(solution)/shard_map/ppermute | solution.py:328
  122.3 3.1 collective-permute-start.33
  129.9 3.1 collective-permute-start.40
  138.4 1.9 slot8_0.1
  141.8 2.4 collective-permute-start.37
  144.2 5.2 %collective-permute-done.41.refs_3_ = f32[344,256]{1,0:T(8,128)S(1)} collective-permute-done((f32[344,256]{1,0:T(8,128)S(1)}, f32[344,256]{1,0:T(8,128)S(1)}, u32[]{:S(2)}, u32[]{:S(2)}) %collective-permute-start.41) | collective-permute-done | bytes 352288 | tf_op jit(solution)/shard_map/ppermute | solution.py:328
  149.3 1.9 slot8_1.1
  151.9 2.0 collective-permute-start.45
  154.0 1.9 slot9_0.1
  156.1 2.5 collective-permute-start.43
  158.6 2.0 collective-permute-done.44.refs_0_
  162.2 1.9 slot9_1.1
  164.1 4.0 %collective-permute-done.42.refs_2_ = f32[344,256]{1,0:T(8,128)S(1)} collective-permute-done((f32[344,256]{1,0:T(8,128)S(1)}, f32[344,256]{1,0:T(8,128)S(1)}, u32[]{:S(2)}, u32[]{:S(2)}) %collective-permute-start.42) | collective-permute-done | bytes 352288 | tf_op jit(solution)/shard_map/ppermute | solution.py:326
  171.5 3.9 regroup.3
  175.4 7.3 %all-to-all-start.1 = ((f32[16,8,8192]{2,1,0:T(8,128)}), f32[16,8,8192]{2,1,0:T(8,128)}, u32[]{:S(2)}, u32[]{:S(2)}) async-start(f32[16,8,8192]{2,1,0:T(8,128)} %regroup.3), calls=%async_computation.1 | async-start | bytes 8388608 | tf_op jit(solution)/shard_map/all_to_all | solution.py:332
  184.7 9.0 %collective-permute-done.52 = f32[256,256]{1,0:T(8,128)S(1)} collective-permute-done((f32[256,256]{1,0:T(8,128)S(1)}, f32[256,256]{1,0:T(8,128)S(1)}, u32[]{:S(2)}, u32[]{:S(2)}) %collective-permute-start.52) | collective-permute-done | bytes 262176 | tf_op jit(solution)/shard_map/ppermute | solution.py:294
  196.0 6.4 %collective-permute-done.53 = f32[256,256]{1,0:T(8,128)S(1)} collective-permute-done((f32[256,256]{1,0:T(8,128)S(1)}, f32[256,256]{1,0:T(8,128)S(1)}, u32[]{:S(2)}, u32[]{:S(2)}) %collective-permute-start.53) | collective-permute-done | bytes 262176 | tf_op jit(solution)/shard_map/ppermute | solution.py:294
  202.4 8.9 %collective-permute-start.54 = (f32[256,256]{1,0:T(8,128)S(1)}, f32[256,256]{1,0:T(8,128)S(1)}, u32[]{:S(2)}, u32[]{:S(2)}) collective-permute-start(f32[256,256]{1,0:T(8,128)S(1)} %add.37), channel_id=1, source_target_pairs={{0,4},{1,5},{2,6},{3,7},{4,0},{5,1},{6,2},{7,3},{8,12},{9,13},{10,... | collective-permute-start | bytes 786440 | tf_op jit(solution)/shard_map/ppermute | solution.py:294
  211.5 2.8 collective-permute-start.59
  214.3 25.4 %collective-permute-done.54 = f32[256,256]{1,0:T(8,128)S(1)} collective-permute-done((f32[256,256]{1,0:T(8,128)S(1)}, f32[256,256]{1,0:T(8,128)S(1)}, u32[]{:S(2)}, u32[]{:S(2)}) %collective-permute-start.54) | collective-permute-done | bytes 262176 | tf_op jit(solution)/shard_map/ppermute | solution.py:294
  240.7 3.0 collective-permute-start.57
  248.5 6.4 %collective-permute-done.59.refs_5_ = f32[344,256]{1,0:T(8,128)S(1)} collective-permute-done((f32[344,256]{1,0:T(8,128)S(1)}, f32[344,256]{1,0:T(8,128)S(1)}, u32[]{:S(2)}, u32[]{:S(2)}) %collective-permute-start.59) | collective-permute-done | bytes 352288 | tf_op jit(solution)/shard_map/ppermute | solution.py:328
  254.9 2.7 collective-permute-start.49
  257.6 1.9 slot11_0.1
  259.6 2.8 collective-permute-done.50.refs_2_
  262.4 2.0 collective-permute-start.63
  264.4 5.5 %collective-permute-done.51.refs_3_ = f32[344,256]{1,0:T(8,128)S(1)} collective-permute-done((f32[344,256]{1,0:T(8,128)S(1)}, f32[344,256]{1,0:T(8,128)S(1)}, u32[]{:S(2)}, u32[]{:S(2)}) %collective-permute-start.51) | collective-permute-done | bytes 352288 | tf_op jit(solution)/shard_map/ppermute | solution.py:328
  270.0 1.9 slot11_1.1
  272.0 2.7 collective-permute-start.61
  276.5 2.7 collective-permute-start.67
  279.1 3.3 collective-permute-done.60.refs_0_
  284.3 2.6 collective-permute-start.65
  286.9 3.0 collective-permute-done.66.refs_2_
  291.9 2.5 collective-permute-start.71
  294.4 3.0 collective-permute-done.64.refs_0_
  299.3 2.7 collective-permute-start.69
  302.0 3.1 collective-permute-done.70.refs_2_
  306.7 5.9 %collective-permute-done.68.refs_0_ = f32[344,256]{1,0:T(8,128)S(1)} collective-permute-done((f32[344,256]{1,0:T(8,128)S(1)}, f32[344,256]{1,0:T(8,128)S(1)}, u32[]{:S(2)}, u32[]{:S(2)}) %collective-permute-start.68) | collective-permute-done | bytes 352288 | tf_op jit(solution)/shard_map/ppermute | solution.py:326
  314.2 20.5 %project.1 = f32[3,256,256]{2,1,0:T(8,128)S(1)} custom-call(f32[128,8192]{1,0:T(8,128)} %bitcast.1.refs_4_.xa_ref, f32[128,8192]{1,0:T(8,128)} %bitcast.2.xb_ref, f32[8192,256]{1,0:T(8,128)} %get-tuple-element.259.p1_ref, f32[8192,256]{1,0:T(8,128)} %get-tuple-element.260.p0_ref), custom_call_target="tpu_custom_call" | custom-call | tf_op jit(solution)/shard_map/project/pallas_call | solution.py:241
  334.7 18.6 %all_to_all.15 = f32[16,48,256]{2,1,0:T(8,128)S(1)} all-to-all(f32[16,48,256]{2,1,0:T(8,128)S(1)} %bitcast.18), channel_id=1, replica_groups=mesh['row'=16,'col'=8] {'row'}, dimensions={0} | all-to-all | bytes 1572864 | tf_op jit(solution)/shard_map/all_to_all | solution.py:338
  353.3 19.7 %all_gather.3 = f32[768,256]{1,0:T(8,128)S(1)} all-gather(f32[48,256]{1,0:T(8,128)S(1)} %reduce_sum.9), channel_id=1, replica_groups=mesh['row'=16,'col'=8] {'row'}, dimensions={0}, use_global_device_ids=true | all-gather | bytes 835584 | tf_op jit(solution)/shard_map/all_gather | solution.py:339
  373.0 20.8 %update.1 = f32[16,2,8,8192]{3,2,1,0:T(8,128)} custom-call(f32[3,256,256]{2,1,0:T(8,128)S(1)} %bitcast.19, f32[256,256]{1,0:T(8,128)S(1)} %get-tuple-element.264.refs_4_.f1_ref, f32[256,256]{1,0:T(8,128)S(1)} %get-tuple-element.263.refs_5_.f0_ref, f32[128,8192]{1,0:T(8,128)} %bitcast.1.refs_4_.xa_ref, f32[128,8192]{1,0:T(8,128)} %bitcast.2.xb_ref, ...), custom_call_target="tpu_custom_call" | custom-call | tf_op jit(solution)/shard_map/update/pallas_call | solution.py:278
  (138 shorter events, 80.7 us)
Async XLA Ops:
  8.8 98.6 %all-to-all-start = ((f32[16,8,8192]{2,1,0:T(8,128)}), f32[16,8,8192]{2,1,0:T(8,128)}, u32[]{:S(2)}, u32[]{:S(2)}) async-start(f32[16,8,8192]{2,1,0:T(8,128)} %regroup.2.refs_4_), calls=%async_computation | async-start | bytes 8388608 | tf_op jit(solution)/shard_map/all_to_all | solution.py:332
  15.6 12.3 %collective-permute-start = (f32[344,256]{1,0:T(8,128)S(1)}, f32[344,256]{1,0:T(8,128)S(1)}, u32[]{:S(2)}, u32[]{:S(2)}) collective-permute-start(f32[344,256]{1,0:T(8,128)S(1)} %get-tuple-element.136), channel_id=1, source_target_pairs={{0,1},{1,2},{2,3},{3,0},{4,5},{5,6},{6,7},{7,4},{8,9},{9,10},{10,1... | collective-permute-start | bytes 1056776 | tf_op jit(solution)/shard_map/ppermute | solution.py:326
  19.4 16.1 %collective-permute-start.4 = (f32[344,256]{1,0:T(8,128)S(1)}, f32[344,256]{1,0:T(8,128)S(1)}, u32[]{:S(2)}, u32[]{:S(2)}) collective-permute-start(f32[344,256]{1,0:T(8,128)S(1)} %get-tuple-element.135.dep_ref), channel_id=1, source_target_pairs={{0,1},{1,2},{2,3},{3,0},{4,5},{5,6},{6,7},{7,4},{8,9},{9,10},{10,1... | collective-permute-start | bytes 1056776 | tf_op jit(solution)/shard_map/ppermute | solution.py:326
  20.2 15.5 %collective-permute-start.5 = (f32[344,256]{1,0:T(8,128)S(1)}, f32[344,256]{1,0:T(8,128)S(1)}, u32[]{:S(2)}, u32[]{:S(2)}) collective-permute-start(f32[344,256]{1,0:T(8,128)S(1)} %get-tuple-element.142), channel_id=1, source_target_pairs={{0,3},{1,0},{2,1},{3,2},{4,7},{5,4},{6,5},{7,6},{8,11},{9,8},{10,9... | collective-permute-start | bytes 1056776 | tf_op jit(solution)/shard_map/ppermute | solution.py:326
  29.1 13.9 %collective-permute-start.2 = (f32[344,256]{1,0:T(8,128)S(1)}, f32[344,256]{1,0:T(8,128)S(1)}, u32[]{:S(2)}, u32[]{:S(2)}) collective-permute-start(f32[344,256]{1,0:T(8,128)S(1)} %get-tuple-element.140), channel_id=1, source_target_pairs={{0,1},{1,2},{2,3},{3,0},{4,5},{5,6},{6,7},{7,4},{8,9},{9,10},{10,1... | collective-permute-start | bytes 1056776 | tf_op jit(solution)/shard_map/ppermute | solution.py:326
  30.2 13.0 %collective-permute-start.3 = (f32[344,256]{1,0:T(8,128)S(1)}, f32[344,256]{1,0:T(8,128)S(1)}, u32[]{:S(2)}, u32[]{:S(2)}) collective-permute-start(f32[344,256]{1,0:T(8,128)S(1)} %get-tuple-element.141), channel_id=1, source_target_pairs={{0,3},{1,0},{2,1},{3,2},{4,7},{5,4},{6,5},{7,6},{8,11},{9,8},{10,9... | collective-permute-start | bytes 1056776 | tf_op jit(solution)/shard_map/ppermute | solution.py:326
  36.7 13.9 %collective-permute-start.8 = (f32[344,256]{1,0:T(8,128)S(1)}, f32[344,256]{1,0:T(8,128)S(1)}, u32[]{:S(2)}, u32[]{:S(2)}) collective-permute-start(f32[344,256]{1,0:T(8,128)S(1)} %get-tuple-element.149), channel_id=1, source_target_pairs={{0,1},{1,2},{2,3},{3,0},{4,5},{5,6},{6,7},{7,4},{8,9},{9,10},{10,1... | collective-permute-start | bytes 1056776 | tf_op jit(solution)/shard_map/ppermute | solution.py:326
  38.5 12.3 %collective-permute-start.9 = (f32[344,256]{1,0:T(8,128)S(1)}, f32[344,256]{1,0:T(8,128)S(1)}, u32[]{:S(2)}, u32[]{:S(2)}) collective-permute-start(f32[344,256]{1,0:T(8,128)S(1)} %get-tuple-element.150), channel_id=1, source_target_pairs={{0,3},{1,0},{2,1},{3,2},{4,7},{5,4},{6,5},{7,6},{8,11},{9,8},{10,9... | collective-permute-start | bytes 1056776 | tf_op jit(solution)/shard_map/ppermute | solution.py:326
  44.2 13.9 %collective-permute-start.6 = (f32[344,256]{1,0:T(8,128)S(1)}, f32[344,256]{1,0:T(8,128)S(1)}, u32[]{:S(2)}, u32[]{:S(2)}) collective-permute-start(f32[344,256]{1,0:T(8,128)S(1)} %get-tuple-element.147), channel_id=1, source_target_pairs={{0,1},{1,2},{2,3},{3,0},{4,5},{5,6},{6,7},{7,4},{8,9},{9,10},{10,1... | collective-permute-start | bytes 1056776 | tf_op jit(solution)/shard_map/ppermute | solution.py:326
  46.0 12.3 %collective-permute-start.7 = (f32[344,256]{1,0:T(8,128)S(1)}, f32[344,256]{1,0:T(8,128)S(1)}, u32[]{:S(2)}, u32[]{:S(2)}) collective-permute-start(f32[344,256]{1,0:T(8,128)S(1)} %get-tuple-element.148), channel_id=1, source_target_pairs={{0,3},{1,0},{2,1},{3,2},{4,7},{5,4},{6,5},{7,6},{8,11},{9,8},{10,9... | collective-permute-start | bytes 1056776 | tf_op jit(solution)/shard_map/ppermute | solution.py:326
  51.8 13.9 %collective-permute-start.12 = (f32[344,256]{1,0:T(8,128)S(1)}, f32[344,256]{1,0:T(8,128)S(1)}, u32[]{:S(2)}, u32[]{:S(2)}) collective-permute-start(f32[344,256]{1,0:T(8,128)S(1)} %get-tuple-element.157), channel_id=1, source_target_pairs={{0,1},{1,2},{2,3},{3,0},{4,5},{5,6},{6,7},{7,4},{8,9},{9,10},{10,1... | collective-permute-start | bytes 1056776 | tf_op jit(solution)/shard_map/ppermute | solution.py:326
  53.6 12.2 %collective-permute-start.13 = (f32[344,256]{1,0:T(8,128)S(1)}, f32[344,256]{1,0:T(8,128)S(1)}, u32[]{:S(2)}, u32[]{:S(2)}) collective-permute-start(f32[344,256]{1,0:T(8,128)S(1)} %get-tuple-element.158), channel_id=1, source_target_pairs={{0,3},{1,0},{2,1},{3,2},{4,7},{5,4},{6,5},{7,6},{8,11},{9,8},{10,9... | collective-permute-start | bytes 1056776 | tf_op jit(solution)/shard_map/ppermute | solution.py:326
  59.9 14.0 %collective-permute-start.10 = (f32[344,256]{1,0:T(8,128)S(1)}, f32[344,256]{1,0:T(8,128)S(1)}, u32[]{:S(2)}, u32[]{:S(2)}) collective-permute-start(f32[344,256]{1,0:T(8,128)S(1)} %get-tuple-element.155), channel_id=1, source_target_pairs={{0,1},{1,2},{2,3},{3,0},{4,5},{5,6},{6,7},{7,4},{8,9},{9,10},{10,1... | collective-permute-start | bytes 1056776 | tf_op jit(solution)/shard_map/ppermute | solution.py:326
  61.3 14.4 %collective-permute-start.11 = (f32[344,256]{1,0:T(8,128)S(1)}, f32[344,256]{1,0:T(8,128)S(1)}, u32[]{:S(2)}, u32[]{:S(2)}) collective-permute-start(f32[344,256]{1,0:T(8,128)S(1)} %get-tuple-element.156), channel_id=1, source_target_pairs={{0,3},{1,0},{2,1},{3,2},{4,7},{5,4},{6,5},{7,6},{8,11},{9,8},{10,9... | collective-permute-start | bytes 1056776 | tf_op jit(solution)/shard_map/ppermute | solution.py:326
  67.3 13.0 %collective-permute-start.18 = (f32[344,256]{1,0:T(8,128)S(1)}, f32[344,256]{1,0:T(8,128)S(1)}, u32[]{:S(2)}, u32[]{:S(2)}) collective-permute-start(f32[344,256]{1,0:T(8,128)S(1)} %get-tuple-element.167), channel_id=1, source_target_pairs={{0,1},{1,2},{2,3},{3,0},{4,5},{5,6},{6,7},{7,4},{8,9},{9,10},{10,1... | collective-permute-start | bytes 1056776 | tf_op jit(solution)/shard_map/ppermute | solution.py:326
  68.8 14.4 %collective-permute-start.19 = (f32[344,256]{1,0:T(8,128)S(1)}, f32[344,256]{1,0:T(8,128)S(1)}, u32[]{:S(2)}, u32[]{:S(2)}) collective-permute-start(f32[344,256]{1,0:T(8,128)S(1)} %get-tuple-element.168), channel_id=1, source_target_pairs={{0,3},{1,0},{2,1},{3,2},{4,7},{5,4},{6,5},{7,6},{8,11},{9,8},{10,9... | collective-permute-start | bytes 1056776 | tf_op jit(solution)/shard_map/ppermute | solution.py:326
  70.1 16.0 %collective-permute-start.16 = (f32[344,256]{1,0:T(8,128)S(1)}, f32[344,256]{1,0:T(8,128)S(1)}, u32[]{:S(2)}, u32[]{:S(2)}) collective-permute-start(f32[344,256]{1,0:T(8,128)S(1)} %get-tuple-element.165), channel_id=1, source_target_pairs={{0,4},{1,5},{2,6},{3,7},{4,0},{5,1},{6,2},{7,3},{8,12},{9,13},{10,... | collective-permute-start | bytes 1056776 | tf_op jit(solution)/shard_map/ppermute | solution.py:328
  73.9 14.3 %collective-permute-start.17 = (f32[344,256]{1,0:T(8,128)S(1)}, f32[344,256]{1,0:T(8,128)S(1)}, u32[]{:S(2)}, u32[]{:S(2)}) collective-permute-start(f32[344,256]{1,0:T(8,128)S(1)} %get-tuple-element.166), channel_id=1, source_target_pairs={{0,4},{1,5},{2,6},{3,7},{4,0},{5,1},{6,2},{7,3},{8,12},{9,13},{10,... | collective-permute-start | bytes 1056776 | tf_op jit(solution)/shard_map/ppermute | solution.py:328
  77.2 11.0 %collective-permute-start.14 = (f32[344,256]{1,0:T(8,128)S(1)}, f32[344,256]{1,0:T(8,128)S(1)}, u32[]{:S(2)}, u32[]{:S(2)}) collective-permute-start(f32[344,256]{1,0:T(8,128)S(1)} %get-tuple-element.163), channel_id=1, source_target_pairs={{0,1},{1,2},{2,3},{3,0},{4,5},{5,6},{6,7},{7,4},{8,9},{9,10},{10,1... | collective-permute-start | bytes 1056776 | tf_op jit(solution)/shard_map/ppermute | solution.py:326
  80.3 15.0 %collective-permute-start.24 = (f32[344,256]{1,0:T(8,128)S(1)}, f32[344,256]{1,0:T(8,128)S(1)}, u32[]{:S(2)}, u32[]{:S(2)}) collective-permute-start(f32[344,256]{1,0:T(8,128)S(1)} %get-tuple-element.177), channel_id=1, source_target_pairs={{0,4},{1,5},{2,6},{3,7},{4,0},{5,1},{6,2},{7,3},{8,12},{9,13},{10,... | collective-permute-start | bytes 1056776 | tf_op jit(solution)/shard_map/ppermute | solution.py:328
  86.1 16.8 %collective-permute-start.25 = (f32[344,256]{1,0:T(8,128)S(1)}, f32[344,256]{1,0:T(8,128)S(1)}, u32[]{:S(2)}, u32[]{:S(2)}) collective-permute-start(f32[344,256]{1,0:T(8,128)S(1)} %get-tuple-element.178), channel_id=1, source_target_pairs={{0,4},{1,5},{2,6},{3,7},{4,0},{5,1},{6,2},{7,3},{8,12},{9,13},{10,... | collective-permute-start | bytes 1056776 | tf_op jit(solution)/shard_map/ppermute | solution.py:328
  88.2 14.6 %collective-permute-start.22 = (f32[344,256]{1,0:T(8,128)S(1)}, f32[344,256]{1,0:T(8,128)S(1)}, u32[]{:S(2)}, u32[]{:S(2)}) collective-permute-start(f32[344,256]{1,0:T(8,128)S(1)} %get-tuple-element.175), channel_id=1, source_target_pairs={{0,1},{1,2},{2,3},{3,0},{4,5},{5,6},{6,7},{7,4},{8,9},{9,10},{10,1... | collective-permute-start | bytes 1056776 | tf_op jit(solution)/shard_map/ppermute | solution.py:326
  88.2 14.6 %collective-permute-start.23 = (f32[344,256]{1,0:T(8,128)S(1)}, f32[344,256]{1,0:T(8,128)S(1)}, u32[]{:S(2)}, u32[]{:S(2)}) collective-permute-start(f32[344,256]{1,0:T(8,128)S(1)} %get-tuple-element.176), channel_id=1, source_target_pairs={{0,3},{1,0},{2,1},{3,2},{4,7},{5,4},{6,5},{7,6},{8,11},{9,8},{10,9... | collective-permute-start | bytes 1056776 | tf_op jit(solution)/shard_map/ppermute | solution.py:326
  92.7 14.6 %collective-permute-start.20 = (f32[344,256]{1,0:T(8,128)S(1)}, f32[344,256]{1,0:T(8,128)S(1)}, u32[]{:S(2)}, u32[]{:S(2)}) collective-permute-start(f32[344,256]{1,0:T(8,128)S(1)} %get-tuple-element.173), channel_id=1, source_target_pairs={{0,1},{1,2},{2,3},{3,0},{4,5},{5,6},{6,7},{7,4},{8,9},{9,10},{10,1... | collective-permute-start | bytes 1056776 | tf_op jit(solution)/shard_map/ppermute | solution.py:326
  95.3 12.0 %collective-permute-start.21 = (f32[344,256]{1,0:T(8,128)S(1)}, f32[344,256]{1,0:T(8,128)S(1)}, u32[]{:S(2)}, u32[]{:S(2)}) collective-permute-start(f32[344,256]{1,0:T(8,128)S(1)} %get-tuple-element.174), channel_id=1, source_target_pairs={{0,3},{1,0},{2,1},{3,2},{4,7},{5,4},{6,5},{7,6},{8,11},{9,8},{10,9... | collective-permute-start | bytes 1056776 | tf_op jit(solution)/shard_map/ppermute | solution.py:326
  109.2 13.1 %collective-permute-start.26 = (f32[344,256]{1,0:T(8,128)S(1)}, f32[344,256]{1,0:T(8,128)S(1)}, u32[]{:S(2)}, u32[]{:S(2)}) collective-permute-start(f32[344,256]{1,0:T(8,128)S(1)} %get-tuple-element.183), channel_id=1, source_target_pairs={{0,1},{1,2},{2,3},{3,0},{4,5},{5,6},{6,7},{7,4},{8,9},{9,10},{10,1... | collective-permute-start | bytes 1056776 | tf_op jit(solution)/shard_map/ppermute | solution.py:326
  109.3 16.1 %collective-permute-start.27 = (f32[344,256]{1,0:T(8,128)S(1)}, f32[344,256]{1,0:T(8,128)S(1)}, u32[]{:S(2)}, u32[]{:S(2)}) collective-permute-start(f32[344,256]{1,0:T(8,128)S(1)} %get-tuple-element.184), channel_id=1, source_target_pairs={{0,3},{1,0},{2,1},{3,2},{4,7},{5,4},{6,5},{7,6},{8,11},{9,8},{10,9... | collective-permute-start | bytes 1056776 | tf_op jit(solution)/shard_map/ppermute | solution.py:326
  115.3 13.0 %collective-permute-start.34 = (f32[344,256]{1,0:T(8,128)S(1)}, f32[344,256]{1,0:T(8,128)S(1)}, u32[]{:S(2)}, u32[]{:S(2)}) collective-permute-start(f32[344,256]{1,0:T(8,128)S(1)} %get-tuple-element.195), channel_id=1, source_target_pairs={{0,1},{1,2},{2,3},{3,0},{4,5},{5,6},{6,7},{7,4},{8,9},{9,10},{10,1... | collective-permute-start | bytes 1056776 | tf_op jit(solution)/shard_map/ppermute | solution.py:326
  115.5 14.3 %collective-permute-start.35 = (f32[344,256]{1,0:T(8,128)S(1)}, f32[344,256]{1,0:T(8,128)S(1)}, u32[]{:S(2)}, u32[]{:S(2)}) collective-permute-start(f32[344,256]{1,0:T(8,128)S(1)} %get-tuple-element.196), channel_id=1, source_target_pairs={{0,3},{1,0},{2,1},{3,2},{4,7},{5,4},{6,5},{7,6},{8,11},{9,8},{10,9... | collective-permute-start | bytes 1056776 | tf_op jit(solution)/shard_map/ppermute | solution.py:326
  118.1 16.6 %collective-permute-start.32 = (f32[344,256]{1,0:T(8,128)S(1)}, f32[344,256]{1,0:T(8,128)S(1)}, u32[]{:S(2)}, u32[]{:S(2)}) collective-permute-start(f32[344,256]{1,0:T(8,128)S(1)} %get-tuple-element.193), channel_id=1, source_target_pairs={{0,4},{1,5},{2,6},{3,7},{4,0},{5,1},{6,2},{7,3},{8,12},{9,13},{10,... | collective-permute-start | bytes 1056776 | tf_op jit(solution)/shard_map/ppermute | solution.py:328
  122.3 13.4 %collective-permute-start.33 = (f32[344,256]{1,0:T(8,128)S(1)}, f32[344,256]{1,0:T(8,128)S(1)}, u32[]{:S(2)}, u32[]{:S(2)}) collective-permute-start(f32[344,256]{1,0:T(8,128)S(1)} %get-tuple-element.194), channel_id=1, source_target_pairs={{0,4},{1,5},{2,6},{3,7},{4,0},{5,1},{6,2},{7,3},{8,12},{9,13},{10,... | collective-permute-start | bytes 1056776 | tf_op jit(solution)/shard_map/ppermute | solution.py:328
  129.9 11.9 %collective-permute-start.40 = (f32[344,256]{1,0:T(8,128)S(1)}, f32[344,256]{1,0:T(8,128)S(1)}, u32[]{:S(2)}, u32[]{:S(2)}) collective-permute-start(f32[344,256]{1,0:T(8,128)S(1)} %get-tuple-element.205), channel_id=1, source_target_pairs={{0,4},{1,5},{2,6},{3,7},{4,0},{5,1},{6,2},{7,3},{8,12},{9,13},{10,... | collective-permute-start | bytes 1056776 | tf_op jit(solution)/shard_map/ppermute | solution.py:328
  134.7 14.6 %collective-permute-start.41 = (f32[344,256]{1,0:T(8,128)S(1)}, f32[344,256]{1,0:T(8,128)S(1)}, u32[]{:S(2)}, u32[]{:S(2)}) collective-permute-start(f32[344,256]{1,0:T(8,128)S(1)} %get-tuple-element.206), channel_id=1, source_target_pairs={{0,4},{1,5},{2,6},{3,7},{4,0},{5,1},{6,2},{7,3},{8,12},{9,13},{10,... | collective-permute-start | bytes 1056776 | tf_op jit(solution)/shard_map/ppermute | solution.py:328
  135.7 13.6 %collective-permute-start.38 = (f32[344,256]{1,0:T(8,128)S(1)}, f32[344,256]{1,0:T(8,128)S(1)}, u32[]{:S(2)}, u32[]{:S(2)}) collective-permute-start(f32[344,256]{1,0:T(8,128)S(1)} %get-tuple-element.203), channel_id=1, source_target_pairs={{0,1},{1,2},{2,3},{3,0},{4,5},{5,6},{6,7},{7,4},{8,9},{9,10},{10,1... | collective-permute-start | bytes 1056776 | tf_op jit(solution)/shard_map/ppermute | solution.py:326
  137.1 12.3 %collective-permute-start.39 = (f32[344,256]{1,0:T(8,128)S(1)}, f32[344,256]{1,0:T(8,128)S(1)}, u32[]{:S(2)}, u32[]{:S(2)}) collective-permute-start(f32[344,256]{1,0:T(8,128)S(1)} %get-tuple-element.204), channel_id=1, source_target_pairs={{0,3},{1,0},{2,1},{3,2},{4,7},{5,4},{6,5},{7,6},{8,11},{9,8},{10,9... | collective-permute-start | bytes 1056776 | tf_op jit(solution)/shard_map/ppermute | solution.py:326
  140.3 13.7 %collective-permute-start.36 = (f32[344,256]{1,0:T(8,128)S(1)}, f32[344,256]{1,0:T(8,128)S(1)}, u32[]{:S(2)}, u32[]{:S(2)}) collective-permute-start(f32[344,256]{1,0:T(8,128)S(1)} %get-tuple-element.201), channel_id=1, source_target_pairs={{0,1},{1,2},{2,3},{3,0},{4,5},{5,6},{6,7},{7,4},{8,9},{9,10},{10,1... | collective-permute-start | bytes 1056776 | tf_op jit(solution)/shard_map/ppermute | solution.py:326
  141.8 12.2 %collective-permute-start.37 = (f32[344,256]{1,0:T(8,128)S(1)}, f32[344,256]{1,0:T(8,128)S(1)}, u32[]{:S(2)}, u32[]{:S(2)}) collective-permute-start(f32[344,256]{1,0:T(8,128)S(1)} %get-tuple-element.202), channel_id=1, source_target_pairs={{0,3},{1,0},{2,1},{3,2},{4,7},{5,4},{6,5},{7,6},{8,11},{9,8},{10,9... | collective-permute-start | bytes 1056776 | tf_op jit(solution)/shard_map/ppermute | solution.py:326
  151.9 10.3 %collective-permute-start.45 = (f32[344,256]{1,0:T(8,128)S(1)}, f32[344,256]{1,0:T(8,128)S(1)}, u32[]{:S(2)}, u32[]{:S(2)}) collective-permute-start(f32[344,256]{1,0:T(8,128)S(1)} %get-tuple-element.214), channel_id=1, source_target_pairs={{0,3},{1,0},{2,1},{3,2},{4,7},{5,4},{6,5},{7,6},{8,11},{9,8},{10,9... | collective-permute-start | bytes 1056776 | tf_op jit(solution)/shard_map/ppermute | solution.py:326
  155.9 12.3 %collective-permute-start.42 = (f32[344,256]{1,0:T(8,128)S(1)}, f32[344,256]{1,0:T(8,128)S(1)}, u32[]{:S(2)}, u32[]{:S(2)}) collective-permute-start(f32[344,256]{1,0:T(8,128)S(1)} %get-tuple-element.211), channel_id=1, source_target_pairs={{0,1},{1,2},{2,3},{3,0},{4,5},{5,6},{6,7},{7,4},{8,9},{9,10},{10,1... | collective-permute-start | bytes 1056776 | tf_op jit(solution)/shard_map/ppermute | solution.py:326
  156.1 13.6 %collective-permute-start.43 = (f32[344,256]{1,0:T(8,128)S(1)}, f32[344,256]{1,0:T(8,128)S(1)}, u32[]{:S(2)}, u32[]{:S(2)}) collective-permute-start(f32[344,256]{1,0:T(8,128)S(1)} %get-tuple-element.212), channel_id=1, source_target_pairs={{0,3},{1,0},{2,1},{3,2},{4,7},{5,4},{6,5},{7,6},{8,11},{9,8},{10,9... | collective-permute-start | bytes 1056776 | tf_op jit(solution)/shard_map/ppermute | solution.py:326
  175.4 138.8 %all-to-all-start.1 = ((f32[16,8,8192]{2,1,0:T(8,128)}), f32[16,8,8192]{2,1,0:T(8,128)}, u32[]{:S(2)}, u32[]{:S(2)}) async-start(f32[16,8,8192]{2,1,0:T(8,128)} %regroup.3), calls=%async_computation.1 | async-start | bytes 8388608 | tf_op jit(solution)/shard_map/all_to_all | solution.py:332
  194.3 45.5 %collective-permute-start.46 = (f32[344,256]{1,0:T(8,128)}, f32[344,256]{1,0:T(8,128)S(1)}, u32[]{:S(2)}, u32[]{:S(2)}) collective-permute-start(f32[344,256]{1,0:T(8,128)} %copy-done.3), channel_id=1, source_target_pairs={{0,1},{1,2},{2,3},{3,0},{4,5},{5,6},{6,7},{7,4},{8,9},{9,10},{10,1... | collective-permute-start | bytes 1056776 | tf_op jit(solution)/shard_map/ppermute | solution.py:326
  202.4 37.4 %collective-permute-start.54 = (f32[256,256]{1,0:T(8,128)S(1)}, f32[256,256]{1,0:T(8,128)S(1)}, u32[]{:S(2)}, u32[]{:S(2)}) collective-permute-start(f32[256,256]{1,0:T(8,128)S(1)} %add.37), channel_id=1, source_target_pairs={{0,4},{1,5},{2,6},{3,7},{4,0},{5,1},{6,2},{7,3},{8,12},{9,13},{10,... | collective-permute-start | bytes 786440 | tf_op jit(solution)/shard_map/ppermute | solution.py:294
  211.3 29.3 %collective-permute-start.47 = (f32[344,256]{1,0:T(8,128)}, f32[344,256]{1,0:T(8,128)S(1)}, u32[]{:S(2)}, u32[]{:S(2)}) collective-permute-start(f32[344,256]{1,0:T(8,128)} %copy-done.2), channel_id=1, source_target_pairs={{0,3},{1,0},{2,1},{3,2},{4,7},{5,4},{6,5},{7,6},{8,11},{9,8},{10,9... | collective-permute-start | bytes 1056776 | tf_op jit(solution)/shard_map/ppermute | solution.py:326
  211.4 36.0 %collective-permute-start.58 = (f32[344,256]{1,0:T(8,128)S(1)}, f32[344,256]{1,0:T(8,128)S(1)}, u32[]{:S(2)}, u32[]{:S(2)}) collective-permute-start(f32[344,256]{1,0:T(8,128)S(1)} %get-tuple-element.229), channel_id=1, source_target_pairs={{0,4},{1,5},{2,6},{3,7},{4,0},{5,1},{6,2},{7,3},{8,12},{9,13},{10,... | collective-permute-start | bytes 1056776 | tf_op jit(solution)/shard_map/ppermute | solution.py:328
  211.5 43.3 %collective-permute-start.59 = (f32[344,256]{1,0:T(8,128)S(1)}, f32[344,256]{1,0:T(8,128)S(1)}, u32[]{:S(2)}, u32[]{:S(2)}) collective-permute-start(f32[344,256]{1,0:T(8,128)S(1)} %get-tuple-element.230), channel_id=1, source_target_pairs={{0,4},{1,5},{2,6},{3,7},{4,0},{5,1},{6,2},{7,3},{8,12},{9,13},{10,... | collective-permute-start | bytes 1056776 | tf_op jit(solution)/shard_map/ppermute | solution.py:328
  239.8 15.1 %collective-permute-start.56 = (f32[344,256]{1,0:T(8,128)S(1)}, f32[344,256]{1,0:T(8,128)S(1)}, u32[]{:S(2)}, u32[]{:S(2)}) collective-permute-start(f32[344,256]{1,0:T(8,128)S(1)} %get-tuple-element.219.dep_ref), channel_id=1, source_target_pairs={{0,1},{1,2},{2,3},{3,0},{4,5},{5,6},{6,7},{7,4},{8,9},{9,10},{10,1... | collective-permute-start | bytes 1056776 | tf_op jit(solution)/shard_map/ppermute | solution.py:326
  240.7 16.9 %collective-permute-start.57 = (f32[344,256]{1,0:T(8,128)S(1)}, f32[344,256]{1,0:T(8,128)S(1)}, u32[]{:S(2)}, u32[]{:S(2)}) collective-permute-start(f32[344,256]{1,0:T(8,128)S(1)} %get-tuple-element.228), channel_id=1, source_target_pairs={{0,3},{1,0},{2,1},{3,2},{4,7},{5,4},{6,5},{7,6},{8,11},{9,8},{10,9... | collective-permute-start | bytes 1056776 | tf_op jit(solution)/shard_map/ppermute | solution.py:326
  245.4 17.0 %collective-permute-start.50 = (f32[344,256]{1,0:T(8,128)S(1)}, f32[344,256]{1,0:T(8,128)S(1)}, u32[]{:S(2)}, u32[]{:S(2)}) collective-permute-start(f32[344,256]{1,0:T(8,128)S(1)} %get-tuple-element.226), channel_id=1, source_target_pairs={{0,4},{1,5},{2,6},{3,7},{4,0},{5,1},{6,2},{7,3},{8,12},{9,13},{10,... | collective-permute-start | bytes 1056776 | tf_op jit(solution)/shard_map/ppermute | solution.py:328
  247.3 22.6 %collective-permute-start.51 = (f32[344,256]{1,0:T(8,128)S(1)}, f32[344,256]{1,0:T(8,128)S(1)}, u32[]{:S(2)}, u32[]{:S(2)}) collective-permute-start(f32[344,256]{1,0:T(8,128)S(1)} %get-tuple-element.227), channel_id=1, source_target_pairs={{0,4},{1,5},{2,6},{3,7},{4,0},{5,1},{6,2},{7,3},{8,12},{9,13},{10,... | collective-permute-start | bytes 1056776 | tf_op jit(solution)/shard_map/ppermute | solution.py:328
  254.9 15.1 %collective-permute-start.48 = (f32[344,256]{1,0:T(8,128)S(1)}, f32[344,256]{1,0:T(8,128)S(1)}, u32[]{:S(2)}, u32[]{:S(2)}) collective-permute-start(f32[344,256]{1,0:T(8,128)S(1)} %get-tuple-element.224), channel_id=1, source_target_pairs={{0,1},{1,2},{2,3},{3,0},{4,5},{5,6},{6,7},{7,4},{8,9},{9,10},{10,1... | collective-permute-start | bytes 1056776 | tf_op jit(solution)/shard_map/ppermute | solution.py:326
  254.9 15.1 %collective-permute-start.49 = (f32[344,256]{1,0:T(8,128)S(1)}, f32[344,256]{1,0:T(8,128)S(1)}, u32[]{:S(2)}, u32[]{:S(2)}) collective-permute-start(f32[344,256]{1,0:T(8,128)S(1)} %get-tuple-element.225), channel_id=1, source_target_pairs={{0,3},{1,0},{2,1},{3,2},{4,7},{5,4},{6,5},{7,6},{8,11},{9,8},{10,9... | collective-permute-start | bytes 1056776 | tf_op jit(solution)/shard_map/ppermute | solution.py:326
  259.5 15.2 %collective-permute-start.62 = (f32[344,256]{1,0:T(8,128)S(1)}, f32[344,256]{1,0:T(8,128)S(1)}, u32[]{:S(2)}, u32[]{:S(2)}) collective-permute-start(f32[344,256]{1,0:T(8,128)S(1)} %get-tuple-element.237), channel_id=1, source_target_pairs={{0,1},{1,2},{2,3},{3,0},{4,5},{5,6},{6,7},{7,4},{8,9},{9,10},{10,1... | collective-permute-start | bytes 1056776 | tf_op jit(solution)/shard_map/ppermute | solution.py:326
  262.4 12.2 %collective-permute-start.63 = (f32[344,256]{1,0:T(8,128)S(1)}, f32[344,256]{1,0:T(8,128)S(1)}, u32[]{:S(2)}, u32[]{:S(2)}) collective-permute-start(f32[344,256]{1,0:T(8,128)S(1)} %get-tuple-element.238), channel_id=1, source_target_pairs={{0,3},{1,0},{2,1},{3,2},{4,7},{5,4},{6,5},{7,6},{8,11},{9,8},{10,9... | collective-permute-start | bytes 1056776 | tf_op jit(solution)/shard_map/ppermute | solution.py:326
  271.9 10.5 %collective-permute-start.60 = (f32[344,256]{1,0:T(8,128)S(1)}, f32[344,256]{1,0:T(8,128)S(1)}, u32[]{:S(2)}, u32[]{:S(2)}) collective-permute-start(f32[344,256]{1,0:T(8,128)S(1)} %get-tuple-element.235), channel_id=1, source_target_pairs={{0,1},{1,2},{2,3},{3,0},{4,5},{5,6},{6,7},{7,4},{8,9},{9,10},{10,1... | collective-permute-start | bytes 1056776 | tf_op jit(solution)/shard_map/ppermute | solution.py:326
  272.0 10.4 %collective-permute-start.61 = (f32[344,256]{1,0:T(8,128)S(1)}, f32[344,256]{1,0:T(8,128)S(1)}, u32[]{:S(2)}, u32[]{:S(2)}) collective-permute-start(f32[344,256]{1,0:T(8,128)S(1)} %get-tuple-element.236), channel_id=1, source_target_pairs={{0,3},{1,0},{2,1},{3,2},{4,7},{5,4},{6,5},{7,6},{8,11},{9,8},{10,9... | collective-permute-start | bytes 1056776 | tf_op jit(solution)/shard_map/ppermute | solution.py:326
  276.4 13.6 %collective-permute-start.66 = (f32[344,256]{1,0:T(8,128)S(1)}, f32[344,256]{1,0:T(8,128)S(1)}, u32[]{:S(2)}, u32[]{:S(2)}) collective-permute-start(f32[344,256]{1,0:T(8,128)S(1)} %get-tuple-element.245), channel_id=1, source_target_pairs={{0,1},{1,2},{2,3},{3,0},{4,5},{5,6},{6,7},{7,4},{8,9},{9,10},{10,1... | collective-permute-start | bytes 1056776 | tf_op jit(solution)/shard_map/ppermute | solution.py:326
  276.5 13.5 %collective-permute-start.67 = (f32[344,256]{1,0:T(8,128)S(1)}, f32[344,256]{1,0:T(8,128)S(1)}, u32[]{:S(2)}, u32[]{:S(2)}) collective-permute-start(f32[344,256]{1,0:T(8,128)S(1)} %get-tuple-element.246), channel_id=1, source_target_pairs={{0,3},{1,0},{2,1},{3,2},{4,7},{5,4},{6,5},{7,6},{8,11},{9,8},{10,9... | collective-permute-start | bytes 1056776 | tf_op jit(solution)/shard_map/ppermute | solution.py:326
  284.2 13.3 %collective-permute-start.64 = (f32[344,256]{1,0:T(8,128)S(1)}, f32[344,256]{1,0:T(8,128)S(1)}, u32[]{:S(2)}, u32[]{:S(2)}) collective-permute-start(f32[344,256]{1,0:T(8,128)S(1)} %get-tuple-element.243), channel_id=1, source_target_pairs={{0,1},{1,2},{2,3},{3,0},{4,5},{5,6},{6,7},{7,4},{8,9},{9,10},{10,1... | collective-permute-start | bytes 1056776 | tf_op jit(solution)/shard_map/ppermute | solution.py:326
  284.3 13.1 %collective-permute-start.65 = (f32[344,256]{1,0:T(8,128)S(1)}, f32[344,256]{1,0:T(8,128)S(1)}, u32[]{:S(2)}, u32[]{:S(2)}) collective-permute-start(f32[344,256]{1,0:T(8,128)S(1)} %get-tuple-element.244), channel_id=1, source_target_pairs={{0,3},{1,0},{2,1},{3,2},{4,7},{5,4},{6,5},{7,6},{8,11},{9,8},{10,9... | collective-permute-start | bytes 1056776 | tf_op jit(solution)/shard_map/ppermute | solution.py:326
  291.7 13.3 %collective-permute-start.70 = (f32[344,256]{1,0:T(8,128)S(1)}, f32[344,256]{1,0:T(8,128)S(1)}, u32[]{:S(2)}, u32[]{:S(2)}) collective-permute-start(f32[344,256]{1,0:T(8,128)S(1)} %get-tuple-element.253), channel_id=1, source_target_pairs={{0,1},{1,2},{2,3},{3,0},{4,5},{5,6},{6,7},{7,4},{8,9},{9,10},{10,1... | collective-permute-start | bytes 1056776 | tf_op jit(solution)/shard_map/ppermute | solution.py:326
  291.9 13.1 %collective-permute-start.71 = (f32[344,256]{1,0:T(8,128)S(1)}, f32[344,256]{1,0:T(8,128)S(1)}, u32[]{:S(2)}, u32[]{:S(2)}) collective-permute-start(f32[344,256]{1,0:T(8,128)S(1)} %get-tuple-element.254), channel_id=1, source_target_pairs={{0,3},{1,0},{2,1},{3,2},{4,7},{5,4},{6,5},{7,6},{8,11},{9,8},{10,9... | collective-permute-start | bytes 1056776 | tf_op jit(solution)/shard_map/ppermute | solution.py:326
  299.2 13.4 %collective-permute-start.68 = (f32[344,256]{1,0:T(8,128)S(1)}, f32[344,256]{1,0:T(8,128)S(1)}, u32[]{:S(2)}, u32[]{:S(2)}) collective-permute-start(f32[344,256]{1,0:T(8,128)S(1)} %get-tuple-element.251), channel_id=1, source_target_pairs={{0,1},{1,2},{2,3},{3,0},{4,5},{5,6},{6,7},{7,4},{8,9},{9,10},{10,1... | collective-permute-start | bytes 1056776 | tf_op jit(solution)/shard_map/ppermute | solution.py:326
  299.3 13.3 %collective-permute-start.69 = (f32[344,256]{1,0:T(8,128)S(1)}, f32[344,256]{1,0:T(8,128)S(1)}, u32[]{:S(2)}, u32[]{:S(2)}) collective-permute-start(f32[344,256]{1,0:T(8,128)S(1)} %get-tuple-element.252), channel_id=1, source_target_pairs={{0,3},{1,0},{2,1},{3,2},{4,7},{5,4},{6,5},{7,6},{8,11},{9,8},{10,9... | collective-permute-start | bytes 1056776 | tf_op jit(solution)/shard_map/ppermute | solution.py:326
  (14 other events, 125.5 us)
where the time goes:
time: 395 us; the launch traced here: 394 us
  waiting for transfers between devices  130 us (33%)
  starting transfers between devices  123 us (31%)
  Pallas kernels  97.7 us (25%)
  blocking collectives  38.3 us (10%)
    ppermute x56, starting transfers between devices, shards(): got[g] = [lax.ppermute(x, 'col', turn) for x, turn in zip(send, turns)]  72.3 us
    ppermute x56, waiting for transfers between devices, shards(): got[g] = [lax.ppermute(x, 'col', turn) for x, turn in zip(send, turns)]  57.2 us
    pallas_call x30, Pallas kernels, slot_call(): pl.pallas_call(functools.partial(slot_body, s, group, len(deps)), out_sha...  48.7 us
    ppermute x3, waiting for transfers between devices, shared_factors(): mine = mine + lax.ppermute(mine, 'col', pairs)  40.8 us
    ppermute x12, waiting for transfers between devices, shards(): crossed[g] = [lax.ppermute(x, 'col', SWAP) for x in across]  32 us
    ppermute x12, starting transfers between devices, shards(): crossed[g] = [lax.ppermute(x, 'col', SWAP) for x in across]  26.4 us
    pallas_call x1, Pallas kernels, update(): pl.pallas_call(update_body, out_shape=jax.ShapeDtypeStruct((groups, 2, ha...  20.8 us
    pallas_call x1, Pallas kernels, project(): pl.pallas_call(project_body, out_shape=jax.ShapeDtypeStruct((3, width, wi...  20.5 us
  transfers between devices with their start and end apart: 74, of which 37 were waited for; matrix products, arithmetic and copies ran while one was open for 0% of the time, Pallas kernels for 11%

commit v1 on v0

v1 whole, which is shorter than its diff:
```python
import functools

import jax
import jax.numpy as jnp
from jax import lax
from jax.experimental import pallas as pl
from jax.experimental.pallas import tpu as pltpu
from jax.sharding import PartitionSpec as P

RING = 4
GROUPS = 2
QUARTER = 3
CHUNKS = RING * QUARTER
SLOTS = max(CHUNKS + 2, 3 * QUARTER + 5)
STEPS = (1, -1)
BLOCKS = (1, 0)
SECOND = (11, 1)
TILE = 2048
VMEM = 48 * 2**20
GRANT = 50 * 2**20
F32 = jnp.float32
ANY = pl.BlockSpec(memory_space=pl.ANY)
HBM = pl.BlockSpec(memory_space=pltpu.HBM)
SMEM = pl.BlockSpec(memory_space=pltpu.SMEM)


def ring_pairs(step):
    return [(h * RING + z, h * RING + (z + step) % RING) for h in range(2) for z in range(RING)]


SWAP = [(i, (i + RING) % (2 * RING)) for i in range(2 * RING)]


def sizes(own, factor):
    part, extra = own.shape[1] // GROUPS, factor.shape[1] // GROUPS
    assert (part + extra) % (CHUNKS * 8) == 0
    return part, extra, (part + extra) // CHUNKS


def crossing_id(batch, place):
    return jnp.where(place == 0, 3 * QUARTER + batch, 3 * batch + 3 - place)


def cross_slots(s):
    send = next((b for b in range(QUARTER) if s == 3 * b + 3), None)
    inject = next((b for b in range(QUARTER) if s == 3 * b + 5), None)
    return send, inject


def plan(s, owner, step):
    me = lax.axis_index("col")
    far = me // RING != owner // RING
    place = jnp.bitwise_and(step * (me - owner), RING - 1)
    source = me == owner
    _, inject = cross_slots(s)
    index = s - place
    keep = (index >= 0) & (index < CHUNKS) & ~far
    if s == 0:
        keep = source
    for b in range(QUARTER):
        j = s - 1 - (3 * b + 5)
        if 0 <= j < 3:
            index = jnp.where(far, crossing_id(b, jnp.bitwise_and(place - 1 - j, RING - 1)), index)
            keep = keep | far
    index = jnp.clip(index, 0, CHUNKS - 1)
    cross = crossing_id(inject, place) if inject is not None else 0
    return source, index, keep, far, cross


def slot_body(s, group, carried, owner_ref, own_ref, factor_ref, *refs):
    refs = list(refs)
    over, inject = cross_slots(s)
    first = s == 0 and group == 0
    none = [None, None]
    heads = [refs.pop(0), refs.pop(0)] if group == 0 else none
    got = [refs.pop(0), refs.pop(0)] if s else none
    crossed = refs.pop(0) if inject is not None else None
    del refs[: carried + (0 if first else 2)]
    held = [refs.pop(0), refs.pop(0)]
    send = [refs.pop(0), refs.pop(0)] if s < SLOTS else none
    across = refs.pop(0) if over is not None else None
    del refs[: len(refs) - 2]
    stage, sems = refs
    part, extra, size = sizes(own_ref, factor_ref)

    now, then = [], []
    for i in range(2):
        source, index, keep, far, cross = plan(s, owner_ref[BLOCKS[i]], STEPS[i])
        both = pl.ds(i * size, size)

        def bring(when, c, to):
            start, stop = c * size, min((c + 1) * size, part)
            if group == 0 and stop <= heads[i].shape[0]:
                now.append((when, heads[i].at[pl.ds(start, size)], to))
                return
            src = own_ref.at[0, pl.ds(group * part + start, stop - start)]
            now.append((when, src, to.at[pl.ds(0, stop - start)]))
            if stop - start < size:
                src = factor_ref.at[0, pl.ds(group * extra, extra)]
                now.append((when, src, to.at[pl.ds(stop - start, extra)]))

        def slot(index):
            return held[i].at[group, pl.ds(pl.multiple_of(index * size, 8), size)]

        here, there = stage.at[i, 0], stage.at[i, 1]
        if s < CHUNKS:
            when = True if s == 0 else source
            bring(when, s, here)
            then.append((when, here, send[i]))
            then.append((source, here, slot(s)))
        passes = ~source if 0 < s < CHUNKS else True
        if inject is not None:
            now.append((far, crossed.at[both], send[i]))
            now.append((far, crossed.at[both], slot(cross)))
            passes = ~far if passes is True else passes & ~far
        if 0 < s < SLOTS:
            now.append((passes, got[i], send[i]))
        if s:
            now.append((keep & ~source, got[i], slot(index)))
        if over is not None:
            bring(source, 3 * QUARTER + over, there)
            then.append((source, there, across.at[both]))
            now.append((~source, got[i], across.at[both]))

    for copies in (now, then):
        for wait in (False, True):
            for n, (when, src, dst) in enumerate(copies):
                copy = pltpu.make_async_copy(src, dst, sems.at[n])
                act = copy.wait if wait else copy.start
                act() if when is True else pl.when(when)(act)


def slot_call(s, group, owner, own, factor, heads, got, crossed, held, wanted=(), carried=None):
    width = own.shape[2]
    part, extra, size = sizes(own, factor)
    over, inject = cross_slots(s)
    ins, specs = [owner, own, factor], [SMEM, HBM, HBM]
    outs, out_specs = [jax.ShapeDtypeStruct((GROUPS, part + extra, width), own.dtype)] * 2, [HBM] * 2
    aliases = {}

    def add(arrays, spec):
        ins.extend(arrays)
        specs.extend([spec] * len(arrays))

    if group == 0:
        add(heads, ANY)
    if s:
        add(got, ANY)
    if inject is not None:
        add([crossed], ANY)
    add(wanted, ANY)
    if carried is not None:
        add([carried], HBM)
    if held is not None:
        aliases = {len(ins): 0, len(ins) + 1: 1}
        add(held, HBM)
    if s < SLOTS:
        outs += [jax.ShapeDtypeStruct((size, width), own.dtype)] * 2
    if over is not None:
        outs += [jax.ShapeDtypeStruct((2 * size, width), own.dtype)]
    out_specs += [ANY] * (len(outs) - 2)
    if carried is not None:
        aliases[len(ins) - 3] = len(outs)
        outs += [jax.ShapeDtypeStruct(carried.shape, carried.dtype)]
        out_specs += [HBM]
    out = pl.pallas_call(
        functools.partial(slot_body, s, group, len(wanted) + (carried is not None)),
        out_shape=outs,
        in_specs=specs,
        out_specs=out_specs,
        scratch_shapes=[pltpu.VMEM((2, 2, size, width), own.dtype), pltpu.SemaphoreType.DMA((20,))],
        input_output_aliases=aliases,
        compiler_params=pltpu.CompilerParams(vmem_limit_bytes=GRANT),
        cost_estimate=pl.CostEstimate(flops=0, bytes_accessed=4 * 2**20, transcendentals=0),
        name=f"slot{s}_{group}",
    )(*ins)
    out = list(out)
    held, out = out[:2], out[2:]
    send = [out.pop(0), out.pop(0)] if s < SLOTS else None
    across = out.pop(0) if over is not None else None
    return held, send, across, out.pop(0) if out else None


def regroup_body(first, groups, x_ref, dep_ref, out_ref, room, sems):
    rows = out_ref.shape[2]

    def come(j):
        src = x_ref.at[0, pl.ds(first, out_ref.shape[1]), pl.ds(j * rows, rows)]
        return pltpu.make_async_copy(src, room.at[j], sems.at[0, j])

    def leave(j):
        return pltpu.make_async_copy(room.at[j], out_ref.at[j], sems.at[1, j])

    for j in range(groups):
        come(j).start()
    for j in range(groups):
        come(j).wait()
        leave(j).start()
    for j in range(groups):
        leave(j).wait()


def regroup(x, first, count, groups, dep):
    shape = (groups, count, x.shape[2] // groups)
    return pl.pallas_call(
        functools.partial(regroup_body, first, groups),
        out_shape=jax.ShapeDtypeStruct(shape, x.dtype),
        in_specs=[HBM, ANY],
        out_specs=HBM,
        scratch_shapes=[pltpu.VMEM(shape, x.dtype), pltpu.SemaphoreType.DMA((2, groups))],
        compiler_params=pltpu.CompilerParams(vmem_limit_bytes=GRANT),
        name="regroup",
    )(x, dep)


def parts_of(x):
    high = x.astype(jnp.bfloat16)
    low = (x - high.astype(F32)).astype(jnp.bfloat16)
    return high, low


def dot3(left, right, dims):
    (lh, ll), (rh, rl) = left, right
    go = functools.partial(lax.dot_general, dimension_numbers=(dims, ((), ())), preferred_element_type=F32)
    return go(lh, rh) + (go(lh, rl) + go(ll, rh))


def full(left, right, dims):
    return lax.dot_general(
        left, right, (dims, ((), ())), precision=lax.Precision.HIGHEST, preferred_element_type=F32
    )


def project_first_body(x_ref, p1_ref, p0_ref, w_ref, gram_ref):
    x, p1, p0 = parts_of(x_ref[...]), parts_of(p1_ref[0]), parts_of(p0_ref[0])

    @pl.when(pl.program_id(0) == 0)
    def _():
        w_ref[...] = jnp.zeros_like(w_ref)
        gram_ref[...] = jnp.zeros_like(gram_ref)

    w_ref[0] += dot3(x, p1, ((1,), (0,)))
    w_ref[1] += dot3(x, p0, ((1,), (0,)))
    gram_ref[...] += dot3(p1, p0, ((0,), (0,)))


def project_second_body(x_ref, p1_ref, p0_ref, first_ref, gram_ref, mine_ref, other_ref, w_ref, sum_ref):
    x, p1, p0 = parts_of(x_ref[...]), parts_of(p1_ref[0]), parts_of(p0_ref[0])

    @pl.when(pl.program_id(0) == 0)
    def _():
        w_ref[...] = jnp.zeros_like(w_ref)

    w_ref[0] += dot3(x, p1, ((1,), (0,)))
    w_ref[1] += dot3(x, p0, ((1,), (0,)))

    @pl.when(pl.program_id(0) == pl.num_programs(0) - 1)
    def _():
        half, width = w_ref.shape[1:]
        for i in range(2):
            sum_ref[pl.ds(2 * i * half, half)] = first_ref[i]
            sum_ref[pl.ds((2 * i + 1) * half, half)] = w_ref[i]
        sum_ref[pl.ds(4 * half, width)] = gram_ref[...]
        core = lax.axis_index("row") % 2
        rows = mine_ref.shape[0]
        mine_ref[...] = sum_ref[pl.ds(pl.multiple_of(core * rows, 8), rows)]
        other_ref[...] = sum_ref[pl.ds(pl.multiple_of((1 - core) * rows, 8), rows)]


def project(fields, held):
    width = held[0].shape[2]
    half, rows = fields[0].shape
    tiles = rows // GROUPS // TILE
    xspec = pl.BlockSpec((half, TILE), lambda i: (0, i))
    pspec = pl.BlockSpec((1, TILE, width), lambda i: (i // tiles, i % tiles, 0))
    whole = pl.BlockSpec(memory_space=pltpu.VMEM)
    w_shape = jax.ShapeDtypeStruct((2, half, width), F32)
    params = pltpu.CompilerParams(vmem_limit_bytes=VMEM)
    first = pl.pallas_call(
        project_first_body,
        out_shape=[w_shape, jax.ShapeDtypeStruct((width, width), F32)],
        grid=(rows // TILE,),
        in_specs=[xspec, pspec, pspec],
        out_specs=[pl.BlockSpec((2, half, width), lambda i: (0, 0, 0)), pl.BlockSpec((width, width), lambda i: (0, 0))],
        compiler_params=params,
        cost_estimate=pl.CostEstimate(flops=6 * rows * width * 2 * width, bytes_accessed=20 * 2**20, transcendentals=0),
        name="project_first",
    )(fields[0], *held)
    count = (4 * half + width) // 2
    return pl.pallas_call(
        project_second_body,
        out_shape=[jax.ShapeDtypeStruct((count, width), F32)] * 2,
        grid=(rows // TILE,),
        in_specs=[xspec, pspec, pspec, whole, whole],
        out_specs=[pl.BlockSpec((count, width), lambda i: (0, 0))] * 2,
        scratch_shapes=[pltpu.VMEM((2, half, width), F32), pltpu.VMEM((2 * count, width), F32)],
        compiler_params=params,
        cost_estimate=pl.CostEstimate(flops=6 * rows * width * width, bytes_accessed=20 * 2**20, transcendentals=0),
        name="project_second",
    )(fields[1], *held, *first)


def row_sum(mine, other):
    devices = lax.axis_size("row")
    pairs = [(i, i ^ 1) for i in range(devices)]
    alike = [[i for i in range(devices) if i % 2 == core] for core in range(2)]
    swap = functools.partial(lax.all_to_all, axis_name="row", split_axis=0, concat_axis=0, tiled=True, axis_index_groups=alike)
    count, width = mine.shape
    chips = devices // 2
    mine = mine + lax.ppermute(other, "row", pairs)
    piece = jnp.sum(swap(mine.reshape(chips, count // chips, width)), 0)
    mine = swap(jnp.broadcast_to(piece, (chips, *piece.shape))).reshape(count, width)
    return mine, lax.ppermute(mine, "row", pairs)


def update_body(mine_ref, other_ref, f1_ref, f0_ref, xa_ref, xb_ref, p1_ref, p0_ref, out_ref, sum_ref, y_ref):
    width = p1_ref.shape[2]

    @pl.when(pl.program_id(0) == 0)
    def _():
        core = lax.axis_index("row") % 2
        rows = mine_ref.shape[0]
        sum_ref[pl.ds(pl.multiple_of(core * rows, 8), rows)] = mine_ref[...]
        sum_ref[pl.ds(pl.multiple_of((1 - core) * rows, 8), rows)] = other_ref[...]
        w1, w0, gram = (sum_ref[pl.ds(i * width, width)] for i in range(3))
        y1 = full(w1, f1_ref[...].reshape(width, width), ((1,), (1,)))
        w0 = w0 - full(y1, gram, ((1,), (0,)))
        y0 = full(w0, f0_ref[...].reshape(width, width), ((1,), (1,)))
        for i, y in enumerate((y1, y0)):
            high, low = parts_of(y)
            y_ref[i, 0] = high
            y_ref[i, 1] = low

    change = 0
    for i, ref in enumerate((p1_ref, p0_ref)):
        change += dot3((y_ref[i, 0], y_ref[i, 1]), parts_of(ref[0]), ((1,), (1,)))
    n, _, sub, rows = out_ref.shape
    for t, ref in enumerate((xa_ref, xb_ref)):
        half = ref.shape[0]
        out_ref[:, t] = (ref[...] - change[t * half : (t + 1) * half]).reshape(n, sub, rows)


def update(mine, other, fields, held, groups):
    width = held[0].shape[2]
    half, rows = fields[0].shape
    tiles = rows // GROUPS // TILE
    xspec = pl.BlockSpec((half, TILE), lambda i: (0, i))
    pspec = pl.BlockSpec((1, TILE, width), lambda i: (i // tiles, i % tiles, 0))
    extra = width // GROUPS
    fspec = pl.BlockSpec((GROUPS, extra, width), lambda i: (0, rows // GROUPS // extra, 0))
    whole = pl.BlockSpec(memory_space=pltpu.VMEM)
    return pl.pallas_call(
        update_body,
        out_shape=jax.ShapeDtypeStruct((groups, 2, half // groups, rows), F32),
        grid=(rows // TILE,),
        in_specs=[whole, whole, fspec, fspec, xspec, xspec, pspec, pspec],
        out_specs=pl.BlockSpec((groups, 2, half // groups, TILE), lambda i: (0, 0, 0, i)),
        scratch_shapes=[
            pltpu.VMEM((2 * mine.shape[0], width), F32),
            pltpu.VMEM((2, 2, width, width), jnp.bfloat16),
        ],
        compiler_params=pltpu.CompilerParams(vmem_limit_bytes=VMEM),
        name="update",
    )(mine, other, *held, *fields, *held)


def shards(eigvecs, reflectors, factors, owner):
    groups = lax.axis_size("row")
    own_count = eigvecs.shape[1]
    rows_here = eigvecs.shape[2] // groups
    width = factors.shape[2]
    half = own_count // 2

    size = sizes(reflectors, factors)[2]
    top = -(-2 * width // size) * size
    heads = []
    for block in BLOCKS:
        rows = lax.axis_index("row") * rows_here + lax.broadcasted_iota(jnp.int32, (top, width), 0)
        cols = lax.broadcasted_iota(jnp.int32, (top, width), 1) + block * width
        head = jnp.where(rows > cols, reflectors[0, :top], 0.0)
        heads.append(jnp.where(rows == cols, 1.0, head))
    held = None
    got = [None] * GROUPS
    crossed = [None] * GROUPS
    turns = [ring_pairs(step) for step in STEPS]
    swap = functools.partial(lax.all_to_all, axis_name="row", split_axis=0, concat_axis=0, tiled=True)
    fields = []
    splits = []
    wanted = {}
    for s in range(SLOTS + 1):
        for g in range(GROUPS):
            held, send, across, carried = slot_call(
                s, g, owner, reflectors, factors, heads, got[g], crossed[g], held,
                wanted.get((s, g), []), splits[1] if (s, g) == SECOND else None,
            )
            if send is not None:
                got[g] = [lax.ppermute(x, "col", turn) for x, turn in zip(send, turns)]
            if across is not None:
                crossed[g] = lax.ppermute(across, "col", SWAP)
            if (s, g) in ((0, GROUPS - 1), (1, GROUPS - 1)):
                splits.append(regroup(eigvecs, len(splits) * half, half, groups, send[0]))
                wanted[s + 1, 0] = [splits[-1]]
            if len(splits) == 1 and not fields:
                fields.append(swap(splits[0]).reshape(groups * half, rows_here))
                wanted[6, 0] = [fields[0]]
            if carried is not None:
                fields.append(swap(carried).reshape(groups * half, rows_here))

    mine, other = row_sum(*project(fields, held))
    return update(mine, other, fields, held, groups).reshape(1, own_count * groups, rows_here)


def solution(mesh):
    in_specs = (P("col", "row", None), P("col", "row", None), P("col", None, None), P())
    out_specs = P("col", None, "row")
    return jax.shard_map(shards, mesh=mesh, in_specs=in_specs, out_specs=out_specs, check_vma=False)
```

time: 395 us -> 342 us (0.87); the launches traced: 394 us -> 335 us
  waiting for transfers between devices: 130 us -> 63.8 us
  Pallas kernels: 97.7 us -> 127 us
  blocking collectives: 38.3 us -> 22.6 us
  starting transfers between devices: 123 us -> 119 us
    ppermute x16 -> x8, waiting for transfers between devices: 72.7 us -> 6.42 us  [the longest x6 3.72 us: shards(): crossed[g] = lax.ppermute(across, 'col', SWAP)]
    pallas_call x31 -> x32, Pallas kernels: 69.1 us -> 103 us  [the longest x30 77.7 us: slot_call(): pl.pallas_call(functools.partial(slot_body, s, group, len(wanted) + (carr...]
    all_gather x1 -> x0, blocking collectives: 19.7 us -> none  [shards(): lax.all_gather(cut, 'row', axis=0, tiled=True).reshape(3, width, width)]
    ppermute x16 -> x8, starting transfers between devices: 36.8 us -> 18.3 us  [the longest x6 14.3 us: shards(): crossed[g] = lax.ppermute(across, 'col', SWAP)]
    all_to_all x2, starting transfers between devices: 14.2 us -> 21.9 us  [the longest x1 15 us: shards(): fields.append(swap(carried).reshape(groups * half, rows_here))]
    ppermute x56, starting transfers between devices: 72.3 us -> 78.4 us  [shards(): got[g] = [lax.ppermute(x, 'col', turn) for x, turn in zip(send, turns)]]
    pallas_call x1, Pallas kernels: 20.8 us -> 15.6 us  [update(): pl.pallas_call(update_body, out_shape=jax.ShapeDtypeStruct((groups, 2, ha...]
    all_to_all x1 -> x2, blocking collectives: 18.6 us -> 22.6 us  [the longest x1 13.3 us: row_sum(): piece = jnp.sum(swap(mine.reshape(chips, count // chips, width)), 0)]
  transfers between devices with their start and end apart: 74 -> 66, of which waited for: 37 -> 26; matrix products, arithmetic and copies ran while one was open for 0% -> 0% of each run, Pallas kernels for 11% -> 26%
where the time goes in v1:
time: 342 us; the launch traced here: 335 us
  Pallas kernels  127 us (37%)
  starting transfers between devices  119 us (35%)
  waiting for transfers between devices  63.8 us (19%)
  blocking collectives  22.6 us (7%)
    ppermute x56, starting transfers between devices, shards(): got[g] = [lax.ppermute(x, 'col', turn) for x, turn in zip(send, turns)]  78.4 us
    pallas_call x30, Pallas kernels, slot_call(): pl.pallas_call(functools.partial(slot_body, s, group, len(wanted) + (carr...  77.7 us
    ppermute x56, waiting for transfers between devices, shards(): got[g] = [lax.ppermute(x, 'col', turn) for x, turn in zip(send, turns)]  57.4 us
    pallas_call x1, Pallas kernels, update(): pl.pallas_call(update_body, out_shape=jax.ShapeDtypeStruct((groups, 2, ha...  15.6 us
    all_to_all x1, starting transfers between devices, shards(): fields.append(swap(carried).reshape(groups * half, rows_here))  15 us
    pallas_call x1, Pallas kernels, project(): pl.pallas_call(project_first_body, out_shape=[w_shape, jax.ShapeDtypeStru...  14.4 us
    ppermute x6, starting transfers between devices, shards(): crossed[g] = lax.ppermute(across, 'col', SWAP)  14.3 us
    all_to_all x1, blocking collectives, row_sum(): piece = jnp.sum(swap(mine.reshape(chips, count // chips, width)), 0)  13.3 us
  transfers between devices with their start and end apart: 66, of which 26 were waited for; matrix products, arithmetic and copies ran while one was open for 0% of the time, Pallas kernels for 26%

profile of v1, /device:TPU:1, one launch (start us, length us, event | category | flops | bytes accessed | tf_op | source)
XLA Modules:
  0.0 335.5 jit_solution(7106116346222980149)
XLA Ops:
  5.1 2.9 slot0_1.1
  8.0 3.9 %regroup.2.refs_4_ = f32[16,8,8192]{2,1,0:T(8,128)} custom-call(f32[1,16,131072]{2,1,0:T(8,128)} %x_ref.3, f32[352,256]{1,0:T(8,128)S(1)} %get-tuple-element.134.dep_ref), custom_call_target="tpu_custom_call" | custom-call | tf_op jit(solution)/shard_map/regroup/pallas_call | solution.py:205
  11.9 6.8 %all-to-all-start = ((f32[16,8,8192]{2,1,0:T(8,128)}), f32[16,8,8192]{2,1,0:T(8,128)}, u32[]{:S(2)}, u32[]{:S(2)}) async-start(f32[16,8,8192]{2,1,0:T(8,128)} %regroup.2.refs_4_), calls=%async_computation | async-start | bytes 8388608 | tf_op jit(solution)/shard_map/all_to_all | solution.py:404
  18.8 2.5 collective-permute-start.3
  22.8 7.0 %collective-permute-done.2.refs_2_ = f32[352,256]{1,0:T(8,128)S(1)} collective-permute-done((f32[352,256]{1,0:T(8,128)S(1)}, f32[352,256]{1,0:T(8,128)S(1)}, u32[]{:S(2)}, u32[]{:S(2)}) %collective-permute-start.2) | collective-permute-done | bytes 360480 | tf_op jit(solution)/shard_map/ppermute | solution.py:397
  31.9 2.7 collective-permute-start.7
  37.5 2.7 slot1_1.1
  41.8 3.8 %regroup.3.refs_4_.refs_3_ = f32[16,8,8192]{2,1,0:T(8,128)} custom-call(f32[1,16,131072]{2,1,0:T(8,128)} %x_ref.3, f32[352,256]{1,0:T(8,128)S(1)} %get-tuple-element.142.dep_ref), custom_call_target="tpu_custom_call" | custom-call | tf_op jit(solution)/shard_map/regroup/pallas_call | solution.py:205
  45.7 2.8 slot2_0.1
  48.6 2.7 collective-permute-start.11
  52.0 2.8 slot2_1.1
  54.8 2.7 collective-permute-start.9
  59.4 3.0 slot3_0.1
  62.5 2.7 collective-permute-start.21
  65.3 2.6 collective-permute-start.15
  67.8 3.0 slot3_1.1
  70.9 2.7 collective-permute-start.13
  74.6 3.1 collective-permute-start.18
  77.7 2.7 slot4_0.1
  83.7 2.8 slot4_1.1
  86.6 2.7 collective-permute-start.17
  89.2 2.9 slot5_0.1
  92.2 3.0 collective-permute-start.25
  95.2 3.7 %collective-permute-done.18.refs_2_ = f32[704,256]{1,0:T(8,128)S(1)} collective-permute-done((f32[704,256]{1,0:T(8,128)S(1)}, f32[704,256]{1,0:T(8,128)S(1)}, u32[]{:S(2)}, u32[]{:S(2)}) %collective-permute-start.18) | collective-permute-done | bytes 720928 | tf_op jit(solution)/shard_map/ppermute | solution.py:399
  98.9 2.9 slot5_1.1
  101.8 2.7 collective-permute-start.23
  104.8 3.0 slot6_0.1
  107.9 3.7 %collective-permute-start.35 = (f32[704,256]{1,0:T(8,128)S(1)}, f32[704,256]{1,0:T(8,128)S(1)}, u32[]{:S(2)}, u32[]{:S(2)}) collective-permute-start(f32[704,256]{1,0:T(8,128)S(1)} %get-tuple-element.197), channel_id=1, source_target_pairs={{0,4},{1,5},{2,6},{3,7},{4,0},{5,1},{6,2},{7,3},{8,12},{9,13},{10,... | collective-permute-start | bytes 2162696 | tf_op jit(solution)/shard_map/ppermute | solution.py:399
  111.7 2.6 collective-permute-start.29
  114.3 3.0 slot6_1.1
  117.4 2.7 collective-permute-start.27
  122.0 2.9 slot7_0.1
  128.9 2.9 slot7_1.1
  131.9 2.7 collective-permute-start.31
  136.0 3.0 slot8_0.1
  139.1 2.7 collective-permute-start.39
  143.4 3.0 slot8_1.1
  146.5 2.7 collective-permute-start.37
  151.2 3.0 slot9_0.1
  156.2 2.5 collective-permute-start.43
  158.8 3.0 slot9_1.1
  161.9 2.7 collective-permute-start.41
  166.6 2.9 slot10_0.1
  169.7 3.8 %collective-permute-done.40.refs_0_ = f32[352,256]{1,0:T(8,128)S(1)} collective-permute-done((f32[352,256]{1,0:T(8,128)S(1)}, f32[352,256]{1,0:T(8,128)S(1)}, u32[]{:S(2)}, u32[]{:S(2)}) %collective-permute-start.40) | collective-permute-done | bytes 360480 | tf_op jit(solution)/shard_map/ppermute | solution.py:397
  173.5 2.9 slot10_1.1
  176.8 10.9 %collective-permute-start.45 = (f32[352,256]{1,0:T(8,128)S(1)}, f32[352,256]{1,0:T(8,128)S(1)}, u32[]{:S(2)}, u32[]{:S(2)}) collective-permute-start(f32[352,256]{1,0:T(8,128)S(1)} %get-tuple-element.219), channel_id=1, source_target_pairs={{0,3},{1,0},{2,1},{3,2},{4,7},{5,4},{6,5},{7,6},{8,11},{9,8},{10,9... | collective-permute-start | bytes 1081352 | tf_op jit(solution)/shard_map/ppermute | solution.py:397
  187.7 3.0 slot11_0.1
  190.8 4.6 %collective-permute-done.45.refs_1_ = f32[352,256]{1,0:T(8,128)S(1)} collective-permute-done((f32[352,256]{1,0:T(8,128)S(1)}, f32[352,256]{1,0:T(8,128)S(1)}, u32[]{:S(2)}, u32[]{:S(2)}) %collective-permute-start.45) | collective-permute-done | bytes 360480 | tf_op jit(solution)/shard_map/ppermute | solution.py:397
  195.3 3.0 slot11_1.1
  198.4 15.0 %all-to-all-start.1 = ((f32[16,8,8192]{2,1,0:T(8,128)}), f32[16,8,8192]{2,1,0:T(8,128)}, u32[]{:S(2)}, u32[]{:S(2)}) async-start(f32[16,8,8192]{2,1,0:T(8,128)} %get-tuple-element.228), calls=%async_computation.1 | async-start | bytes 8388608 | tf_op jit(solution)/shard_map/all_to_all | solution.py:407
  213.4 2.7 collective-permute-start.53
  216.1 2.7 collective-permute-start.51
  218.8 5.8 %collective-permute-done.52.refs_2_ = f32[352,256]{1,0:T(8,128)S(1)} collective-permute-done((f32[352,256]{1,0:T(8,128)S(1)}, f32[352,256]{1,0:T(8,128)S(1)}, u32[]{:S(2)}, u32[]{:S(2)}) %collective-permute-start.52) | collective-permute-done | bytes 360480 | tf_op jit(solution)/shard_map/ppermute | solution.py:397
  228.9 3.3 collective-permute-done.50.refs_0_
  236.7 3.3 collective-permute-done.56.refs_2_
  244.4 3.3 collective-permute-done.54.refs_0_
  252.1 3.3 collective-permute-done.60.refs_2_
  256.9 6.2 %collective-permute-done.58.refs_0_ = f32[352,256]{1,0:T(8,128)S(1)} collective-permute-done((f32[352,256]{1,0:T(8,128)S(1)}, f32[352,256]{1,0:T(8,128)S(1)}, u32[]{:S(2)}, u32[]{:S(2)}) %collective-permute-start.58) | collective-permute-done | bytes 360480 | tf_op jit(solution)/shard_map/ppermute | solution.py:397
  264.7 14.4 %project_first.1 = (f32[2,128,256]{2,1,0:T(8,128)S(1)}, f32[256,256]{1,0:T(8,128)S(1)}) custom-call(f32[128,8192]{1,0:T(8,128)} %bitcast.1.refs_4_.x_ref.xa_ref, f32[2,4224,256]{2,1,0:T(8,128)} %get-tuple-element.253.p1_ref.f1_ref, f32[2,4224,256]{2,1,0:T(8,128)} %get-tuple-element.254.p0_ref.f0_ref), custom_call_target="tpu_custom_call" | custom-call | flops 6442450944 | bytes 20971520 | tf_op jit(solution)/shard_map/project_first/pallas_call | solution.py:279
  279.1 11.2 %project_second.1 = (f32[384,256]{1,0:T(8,128)S(1)}, f32[384,256]{1,0:T(8,128)S(1)}) custom-call(f32[128,8192]{1,0:T(8,128)} %bitcast.2.x_ref.xb_ref, f32[2,4224,256]{2,1,0:T(8,128)} %get-tuple-element.253.p1_ref.f1_ref, f32[2,4224,256]{2,1,0:T(8,128)} %get-tuple-element.254.p0_ref.f0_ref, f32[2,128,256]{2,1,0:T(8,128)S(1)} %get-tuple-element.255.first_ref, ...), custom_call_target="tpu_custom_call" | custom-call | flops 3221225472 | bytes 20971520 | tf_op jit(solution)/shard_map/project_second/pallas_call | solution.py:290
  292.7 13.3 %all_to_all.20 = f32[8,48,256]{2,1,0:T(8,128)S(1)} all-to-all(f32[8,48,256]{2,1,0:T(8,128)S(1)} %bitcast.14), channel_id=1, replica_groups={{0,16,32,48,64,80,96,112},{8,24,40,56,72,88,104,120},{1,17,33,49,65,81,..., dimensions={0} | all-to-all | bytes 786432 | tf_op jit(solution)/shard_map/all_to_all | solution.py:311
  306.0 9.3 %all_to_all.21 = f32[8,48,256]{2,1,0:T(8,128)S(1)} all-to-all(f32[8,48,256]{2,1,0:T(8,128)S(1)} %broadcast_in_dim.15), channel_id=1, replica_groups={{0,16,32,48,64,80,96,112},{8,24,40,56,72,88,104,120},{1,17,33,49,65,81,..., dimensions={0} | all-to-all | bytes 786432 | tf_op jit(solution)/shard_map/all_to_all | solution.py:312
  315.3 3.0 collective-permute-start.63
  319.6 15.6 %update.1 = f32[16,2,8,8192]{3,2,1,0:T(8,128)} custom-call(f32[384,256]{1,0:T(8,128)S(1)} %bitcast.13, f32[384,256]{1,0:T(8,128)S(1)} %collective-permute-done.63.other_ref, f32[2,4224,256]{2,1,0:T(8,128)} %get-tuple-element.253.p1_ref.f1_ref, f32[2,4224,256]{2,1,0:T(8,128)} %get-tuple-element.254.p0_ref.f0_ref, f32[128,8192]{1,0:T(8,128)} %bitcast.1.refs_4_.x_ref.xa_ref, ...), custom_call_target="tpu_custom_call" | custom-call | tf_op jit(solution)/shard_map/update/pallas_call | solution.py:352
  (119 shorter events, 61.7 us)
Async XLA Ops:
  11.9 93.0 %all-to-all-start = ((f32[16,8,8192]{2,1,0:T(8,128)}), f32[16,8,8192]{2,1,0:T(8,128)}, u32[]{:S(2)}, u32[]{:S(2)}) async-start(f32[16,8,8192]{2,1,0:T(8,128)} %regroup.2.refs_4_), calls=%async_computation | async-start | bytes 8388608 | tf_op jit(solution)/shard_map/all_to_all | solution.py:404
  18.7 11.1 %collective-permute-start.2 = (f32[352,256]{1,0:T(8,128)S(1)}, f32[352,256]{1,0:T(8,128)S(1)}, u32[]{:S(2)}, u32[]{:S(2)}) collective-permute-start(f32[352,256]{1,0:T(8,128)S(1)} %get-tuple-element.136), channel_id=1, source_target_pairs={{0,1},{1,2},{2,3},{3,0},{4,5},{5,6},{6,7},{7,4},{8,9},{9,10},{10,1... | collective-permute-start | bytes 1081352 | tf_op jit(solution)/shard_map/ppermute | solution.py:397
  18.8 11.0 %collective-permute-start.3 = (f32[352,256]{1,0:T(8,128)S(1)}, f32[352,256]{1,0:T(8,128)S(1)}, u32[]{:S(2)}, u32[]{:S(2)}) collective-permute-start(f32[352,256]{1,0:T(8,128)S(1)} %get-tuple-element.137), channel_id=1, source_target_pairs={{0,3},{1,0},{2,1},{3,2},{4,7},{5,4},{6,5},{7,6},{8,11},{9,8},{10,9... | collective-permute-start | bytes 1081352 | tf_op jit(solution)/shard_map/ppermute | solution.py:397
  21.4 15.1 %collective-permute-start.1 = (f32[352,256]{1,0:T(8,128)S(1)}, f32[352,256]{1,0:T(8,128)S(1)}, u32[]{:S(2)}, u32[]{:S(2)}) collective-permute-start(f32[352,256]{1,0:T(8,128)S(1)} %get-tuple-element.135), channel_id=1, source_target_pairs={{0,3},{1,0},{2,1},{3,2},{4,7},{5,4},{6,5},{7,6},{8,11},{9,8},{10,9... | collective-permute-start | bytes 1081352 | tf_op jit(solution)/shard_map/ppermute | solution.py:397
  22.4 15.1 %collective-permute-start = (f32[352,256]{1,0:T(8,128)S(1)}, f32[352,256]{1,0:T(8,128)S(1)}, u32[]{:S(2)}, u32[]{:S(2)}) collective-permute-start(f32[352,256]{1,0:T(8,128)S(1)} %get-tuple-element.134.dep_ref), channel_id=1, source_target_pairs={{0,1},{1,2},{2,3},{3,0},{4,5},{5,6},{6,7},{7,4},{8,9},{9,10},{10,1... | collective-permute-start | bytes 1081352 | tf_op jit(solution)/shard_map/ppermute | solution.py:397
  31.8 13.9 %collective-permute-start.6 = (f32[352,256]{1,0:T(8,128)S(1)}, f32[352,256]{1,0:T(8,128)S(1)}, u32[]{:S(2)}, u32[]{:S(2)}) collective-permute-start(f32[352,256]{1,0:T(8,128)S(1)} %get-tuple-element.144), channel_id=1, source_target_pairs={{0,1},{1,2},{2,3},{3,0},{4,5},{5,6},{6,7},{7,4},{8,9},{9,10},{10,1... | collective-permute-start | bytes 1081352 | tf_op jit(solution)/shard_map/ppermute | solution.py:397
  31.9 13.8 %collective-permute-start.7 = (f32[352,256]{1,0:T(8,128)S(1)}, f32[352,256]{1,0:T(8,128)S(1)}, u32[]{:S(2)}, u32[]{:S(2)}) collective-permute-start(f32[352,256]{1,0:T(8,128)S(1)} %get-tuple-element.145), channel_id=1, source_target_pairs={{0,3},{1,0},{2,1},{3,2},{4,7},{5,4},{6,5},{7,6},{8,11},{9,8},{10,9... | collective-permute-start | bytes 1081352 | tf_op jit(solution)/shard_map/ppermute | solution.py:397
  40.3 11.7 %collective-permute-start.5 = (f32[352,256]{1,0:T(8,128)S(1)}, f32[352,256]{1,0:T(8,128)S(1)}, u32[]{:S(2)}, u32[]{:S(2)}) collective-permute-start(f32[352,256]{1,0:T(8,128)S(1)} %get-tuple-element.143), channel_id=1, source_target_pairs={{0,3},{1,0},{2,1},{3,2},{4,7},{5,4},{6,5},{7,6},{8,11},{9,8},{10,9... | collective-permute-start | bytes 1081352 | tf_op jit(solution)/shard_map/ppermute | solution.py:397
  41.8 10.2 %collective-permute-start.4 = (f32[352,256]{1,0:T(8,128)S(1)}, f32[352,256]{1,0:T(8,128)S(1)}, u32[]{:S(2)}, u32[]{:S(2)}) collective-permute-start(f32[352,256]{1,0:T(8,128)S(1)} %get-tuple-element.142.dep_ref), channel_id=1, source_target_pairs={{0,1},{1,2},{2,3},{3,0},{4,5},{5,6},{6,7},{7,4},{8,9},{9,10},{10,1... | collective-permute-start | bytes 1081352 | tf_op jit(solution)/shard_map/ppermute | solution.py:397
  48.5 10.9 %collective-permute-start.10 = (f32[352,256]{1,0:T(8,128)S(1)}, f32[352,256]{1,0:T(8,128)S(1)}, u32[]{:S(2)}, u32[]{:S(2)}) collective-permute-start(f32[352,256]{1,0:T(8,128)S(1)} %get-tuple-element.152), channel_id=1, source_target_pairs={{0,1},{1,2},{2,3},{3,0},{4,5},{5,6},{6,7},{7,4},{8,9},{9,10},{10,1... | collective-permute-start | bytes 1081352 | tf_op jit(solution)/shard_map/ppermute | solution.py:397
  48.6 10.9 %collective-permute-start.11 = (f32[352,256]{1,0:T(8,128)S(1)}, f32[352,256]{1,0:T(8,128)S(1)}, u32[]{:S(2)}, u32[]{:S(2)}) collective-permute-start(f32[352,256]{1,0:T(8,128)S(1)} %get-tuple-element.153), channel_id=1, source_target_pairs={{0,3},{1,0},{2,1},{3,2},{4,7},{5,4},{6,5},{7,6},{8,11},{9,8},{10,9... | collective-permute-start | bytes 1081352 | tf_op jit(solution)/shard_map/ppermute | solution.py:397
  54.7 13.1 %collective-permute-start.8 = (f32[352,256]{1,0:T(8,128)S(1)}, f32[352,256]{1,0:T(8,128)S(1)}, u32[]{:S(2)}, u32[]{:S(2)}) collective-permute-start(f32[352,256]{1,0:T(8,128)S(1)} %get-tuple-element.150), channel_id=1, source_target_pairs={{0,1},{1,2},{2,3},{3,0},{4,5},{5,6},{6,7},{7,4},{8,9},{9,10},{10,1... | collective-permute-start | bytes 1081352 | tf_op jit(solution)/shard_map/ppermute | solution.py:397
  54.8 13.0 %collective-permute-start.9 = (f32[352,256]{1,0:T(8,128)S(1)}, f32[352,256]{1,0:T(8,128)S(1)}, u32[]{:S(2)}, u32[]{:S(2)}) collective-permute-start(f32[352,256]{1,0:T(8,128)S(1)} %get-tuple-element.151), channel_id=1, source_target_pairs={{0,3},{1,0},{2,1},{3,2},{4,7},{5,4},{6,5},{7,6},{8,11},{9,8},{10,9... | collective-permute-start | bytes 1081352 | tf_op jit(solution)/shard_map/ppermute | solution.py:397
  62.4 12.1 %collective-permute-start.14 = (f32[352,256]{1,0:T(8,128)S(1)}, f32[352,256]{1,0:T(8,128)S(1)}, u32[]{:S(2)}, u32[]{:S(2)}) collective-permute-start(f32[352,256]{1,0:T(8,128)S(1)} %get-tuple-element.160), channel_id=1, source_target_pairs={{0,1},{1,2},{2,3},{3,0},{4,5},{5,6},{6,7},{7,4},{8,9},{9,10},{10,1... | collective-permute-start | bytes 1081352 | tf_op jit(solution)/shard_map/ppermute | solution.py:397
  62.5 24.0 %collective-permute-start.21 = (f32[704,256]{1,0:T(8,128)S(1)}, f32[704,256]{1,0:T(8,128)S(1)}, u32[]{:S(2)}, u32[]{:S(2)}) collective-permute-start(f32[704,256]{1,0:T(8,128)S(1)} %get-tuple-element.171), channel_id=1, source_target_pairs={{0,4},{1,5},{2,6},{3,7},{4,0},{5,1},{6,2},{7,3},{8,12},{9,13},{10,... | collective-permute-start | bytes 2162696 | tf_op jit(solution)/shard_map/ppermute | solution.py:399
  65.3 12.4 %collective-permute-start.15 = (f32[352,256]{1,0:T(8,128)S(1)}, f32[352,256]{1,0:T(8,128)S(1)}, u32[]{:S(2)}, u32[]{:S(2)}) collective-permute-start(f32[352,256]{1,0:T(8,128)S(1)} %get-tuple-element.161), channel_id=1, source_target_pairs={{0,3},{1,0},{2,1},{3,2},{4,7},{5,4},{6,5},{7,6},{8,11},{9,8},{10,9... | collective-permute-start | bytes 1081352 | tf_op jit(solution)/shard_map/ppermute | solution.py:397
  70.9 11.2 %collective-permute-start.12 = (f32[352,256]{1,0:T(8,128)S(1)}, f32[352,256]{1,0:T(8,128)S(1)}, u32[]{:S(2)}, u32[]{:S(2)}) collective-permute-start(f32[352,256]{1,0:T(8,128)S(1)} %get-tuple-element.158), channel_id=1, source_target_pairs={{0,1},{1,2},{2,3},{3,0},{4,5},{5,6},{6,7},{7,4},{8,9},{9,10},{10,1... | collective-permute-start | bytes 1081352 | tf_op jit(solution)/shard_map/ppermute | solution.py:397
  70.9 12.7 %collective-permute-start.13 = (f32[352,256]{1,0:T(8,128)S(1)}, f32[352,256]{1,0:T(8,128)S(1)}, u32[]{:S(2)}, u32[]{:S(2)}) collective-permute-start(f32[352,256]{1,0:T(8,128)S(1)} %get-tuple-element.159), channel_id=1, source_target_pairs={{0,3},{1,0},{2,1},{3,2},{4,7},{5,4},{6,5},{7,6},{8,11},{9,8},{10,9... | collective-permute-start | bytes 1081352 | tf_op jit(solution)/shard_map/ppermute | solution.py:397
  74.6 24.3 %collective-permute-start.18 = (f32[704,256]{1,0:T(8,128)S(1)}, f32[704,256]{1,0:T(8,128)S(1)}, u32[]{:S(2)}, u32[]{:S(2)}) collective-permute-start(f32[704,256]{1,0:T(8,128)S(1)} %get-tuple-element.168), channel_id=1, source_target_pairs={{0,4},{1,5},{2,6},{3,7},{4,0},{5,1},{6,2},{7,3},{8,12},{9,13},{10,... | collective-permute-start | bytes 2162696 | tf_op jit(solution)/shard_map/ppermute | solution.py:399
  80.4 8.8 %collective-permute-start.19 = (f32[352,256]{1,0:T(8,128)S(1)}, f32[352,256]{1,0:T(8,128)S(1)}, u32[]{:S(2)}, u32[]{:S(2)}) collective-permute-start(f32[352,256]{1,0:T(8,128)S(1)} %get-tuple-element.169), channel_id=1, source_target_pairs={{0,1},{1,2},{2,3},{3,0},{4,5},{5,6},{6,7},{7,4},{8,9},{9,10},{10,1... | collective-permute-start | bytes 1081352 | tf_op jit(solution)/shard_map/ppermute | solution.py:397
  82.0 7.2 %collective-permute-start.20 = (f32[352,256]{1,0:T(8,128)S(1)}, f32[352,256]{1,0:T(8,128)S(1)}, u32[]{:S(2)}, u32[]{:S(2)}) collective-permute-start(f32[352,256]{1,0:T(8,128)S(1)} %get-tuple-element.170), channel_id=1, source_target_pairs={{0,3},{1,0},{2,1},{3,2},{4,7},{5,4},{6,5},{7,6},{8,11},{9,8},{10,9... | collective-permute-start | bytes 1081352 | tf_op jit(solution)/shard_map/ppermute | solution.py:397
  86.5 12.4 %collective-permute-start.16 = (f32[352,256]{1,0:T(8,128)S(1)}, f32[352,256]{1,0:T(8,128)S(1)}, u32[]{:S(2)}, u32[]{:S(2)}) collective-permute-start(f32[352,256]{1,0:T(8,128)S(1)} %get-tuple-element.166), channel_id=1, source_target_pairs={{0,1},{1,2},{2,3},{3,0},{4,5},{5,6},{6,7},{7,4},{8,9},{9,10},{10,1... | collective-permute-start | bytes 1081352 | tf_op jit(solution)/shard_map/ppermute | solution.py:397
  86.6 12.3 %collective-permute-start.17 = (f32[352,256]{1,0:T(8,128)S(1)}, f32[352,256]{1,0:T(8,128)S(1)}, u32[]{:S(2)}, u32[]{:S(2)}) collective-permute-start(f32[352,256]{1,0:T(8,128)S(1)} %get-tuple-element.167), channel_id=1, source_target_pairs={{0,3},{1,0},{2,1},{3,2},{4,7},{5,4},{6,5},{7,6},{8,11},{9,8},{10,9... | collective-permute-start | bytes 1081352 | tf_op jit(solution)/shard_map/ppermute | solution.py:397
  92.1 12.4 %collective-permute-start.24 = (f32[352,256]{1,0:T(8,128)S(1)}, f32[352,256]{1,0:T(8,128)S(1)}, u32[]{:S(2)}, u32[]{:S(2)}) collective-permute-start(f32[352,256]{1,0:T(8,128)S(1)} %get-tuple-element.178), channel_id=1, source_target_pairs={{0,1},{1,2},{2,3},{3,0},{4,5},{5,6},{6,7},{7,4},{8,9},{9,10},{10,1... | collective-permute-start | bytes 1081352 | tf_op jit(solution)/shard_map/ppermute | solution.py:397
  92.2 12.6 %collective-permute-start.25 = (f32[352,256]{1,0:T(8,128)S(1)}, f32[352,256]{1,0:T(8,128)S(1)}, u32[]{:S(2)}, u32[]{:S(2)}) collective-permute-start(f32[352,256]{1,0:T(8,128)S(1)} %get-tuple-element.179), channel_id=1, source_target_pairs={{0,3},{1,0},{2,1},{3,2},{4,7},{5,4},{6,5},{7,6},{8,11},{9,8},{10,9... | collective-permute-start | bytes 1081352 | tf_op jit(solution)/shard_map/ppermute | solution.py:397
  101.8 12.5 %collective-permute-start.22 = (f32[352,256]{1,0:T(8,128)}, f32[352,256]{1,0:T(8,128)S(1)}, u32[]{:S(2)}, u32[]{:S(2)}) collective-permute-start(f32[352,256]{1,0:T(8,128)} %get-tuple-element.176), channel_id=1, source_target_pairs={{0,1},{1,2},{2,3},{3,0},{4,5},{5,6},{6,7},{7,4},{8,9},{9,10},{10,1... | collective-permute-start | bytes 1081352 | tf_op jit(solution)/shard_map/ppermute | solution.py:397
  101.8 12.4 %collective-permute-start.23 = (f32[352,256]{1,0:T(8,128)S(1)}, f32[352,256]{1,0:T(8,128)S(1)}, u32[]{:S(2)}, u32[]{:S(2)}) collective-permute-start(f32[352,256]{1,0:T(8,128)S(1)} %get-tuple-element.177), channel_id=1, source_target_pairs={{0,3},{1,0},{2,1},{3,2},{4,7},{5,4},{6,5},{7,6},{8,11},{9,8},{10,9... | collective-permute-start | bytes 1081352 | tf_op jit(solution)/shard_map/ppermute | solution.py:397
  107.9 12.2 %collective-permute-start.28 = (f32[352,256]{1,0:T(8,128)S(1)}, f32[352,256]{1,0:T(8,128)S(1)}, u32[]{:S(2)}, u32[]{:S(2)}) collective-permute-start(f32[352,256]{1,0:T(8,128)S(1)} %get-tuple-element.186), channel_id=1, source_target_pairs={{0,1},{1,2},{2,3},{3,0},{4,5},{5,6},{6,7},{7,4},{8,9},{9,10},{10,1... | collective-permute-start | bytes 1081352 | tf_op jit(solution)/shard_map/ppermute | solution.py:397
  107.9 23.9 %collective-permute-start.35 = (f32[704,256]{1,0:T(8,128)S(1)}, f32[704,256]{1,0:T(8,128)S(1)}, u32[]{:S(2)}, u32[]{:S(2)}) collective-permute-start(f32[704,256]{1,0:T(8,128)S(1)} %get-tuple-element.197), channel_id=1, source_target_pairs={{0,4},{1,5},{2,6},{3,7},{4,0},{5,1},{6,2},{7,3},{8,12},{9,13},{10,... | collective-permute-start | bytes 2162696 | tf_op jit(solution)/shard_map/ppermute | solution.py:399
  111.7 10.3 %collective-permute-start.29 = (f32[352,256]{1,0:T(8,128)S(1)}, f32[352,256]{1,0:T(8,128)S(1)}, u32[]{:S(2)}, u32[]{:S(2)}) collective-permute-start(f32[352,256]{1,0:T(8,128)S(1)} %get-tuple-element.187), channel_id=1, source_target_pairs={{0,3},{1,0},{2,1},{3,2},{4,7},{5,4},{6,5},{7,6},{8,11},{9,8},{10,9... | collective-permute-start | bytes 1081352 | tf_op jit(solution)/shard_map/ppermute | solution.py:397
  117.3 9.6 %collective-permute-start.26 = (f32[352,256]{1,0:T(8,128)S(1)}, f32[352,256]{1,0:T(8,128)S(1)}, u32[]{:S(2)}, u32[]{:S(2)}) collective-permute-start(f32[352,256]{1,0:T(8,128)S(1)} %get-tuple-element.184), channel_id=1, source_target_pairs={{0,1},{1,2},{2,3},{3,0},{4,5},{5,6},{6,7},{7,4},{8,9},{9,10},{10,1... | collective-permute-start | bytes 1081352 | tf_op jit(solution)/shard_map/ppermute | solution.py:397
  117.4 11.5 %collective-permute-start.27 = (f32[352,256]{1,0:T(8,128)S(1)}, f32[352,256]{1,0:T(8,128)S(1)}, u32[]{:S(2)}, u32[]{:S(2)}) collective-permute-start(f32[352,256]{1,0:T(8,128)S(1)} %get-tuple-element.185), channel_id=1, source_target_pairs={{0,3},{1,0},{2,1},{3,2},{4,7},{5,4},{6,5},{7,6},{8,11},{9,8},{10,9... | collective-permute-start | bytes 1081352 | tf_op jit(solution)/shard_map/ppermute | solution.py:397
  120.0 21.7 %collective-permute-start.32 = (f32[704,256]{1,0:T(8,128)S(1)}, f32[704,256]{1,0:T(8,128)S(1)}, u32[]{:S(2)}, u32[]{:S(2)}) collective-permute-start(f32[704,256]{1,0:T(8,128)S(1)} %get-tuple-element.194), channel_id=1, source_target_pairs={{0,4},{1,5},{2,6},{3,7},{4,0},{5,1},{6,2},{7,3},{8,12},{9,13},{10,... | collective-permute-start | bytes 2162696 | tf_op jit(solution)/shard_map/ppermute | solution.py:399
  125.0 10.9 %collective-permute-start.33 = (f32[352,256]{1,0:T(8,128)S(1)}, f32[352,256]{1,0:T(8,128)S(1)}, u32[]{:S(2)}, u32[]{:S(2)}) collective-permute-start(f32[352,256]{1,0:T(8,128)S(1)} %get-tuple-element.195), channel_id=1, source_target_pairs={{0,1},{1,2},{2,3},{3,0},{4,5},{5,6},{6,7},{7,4},{8,9},{9,10},{10,1... | collective-permute-start | bytes 1081352 | tf_op jit(solution)/shard_map/ppermute | solution.py:397
  126.9 9.1 %collective-permute-start.34 = (f32[352,256]{1,0:T(8,128)S(1)}, f32[352,256]{1,0:T(8,128)S(1)}, u32[]{:S(2)}, u32[]{:S(2)}) collective-permute-start(f32[352,256]{1,0:T(8,128)S(1)} %get-tuple-element.196), channel_id=1, source_target_pairs={{0,3},{1,0},{2,1},{3,2},{4,7},{5,4},{6,5},{7,6},{8,11},{9,8},{10,9... | collective-permute-start | bytes 1081352 | tf_op jit(solution)/shard_map/ppermute | solution.py:397
  131.8 11.6 %collective-permute-start.30 = (f32[352,256]{1,0:T(8,128)S(1)}, f32[352,256]{1,0:T(8,128)S(1)}, u32[]{:S(2)}, u32[]{:S(2)}) collective-permute-start(f32[352,256]{1,0:T(8,128)S(1)} %get-tuple-element.192), channel_id=1, source_target_pairs={{0,1},{1,2},{2,3},{3,0},{4,5},{5,6},{6,7},{7,4},{8,9},{9,10},{10,1... | collective-permute-start | bytes 1081352 | tf_op jit(solution)/shard_map/ppermute | solution.py:397
  131.9 11.5 %collective-permute-start.31 = (f32[352,256]{1,0:T(8,128)S(1)}, f32[352,256]{1,0:T(8,128)S(1)}, u32[]{:S(2)}, u32[]{:S(2)}) collective-permute-start(f32[352,256]{1,0:T(8,128)S(1)} %get-tuple-element.193), channel_id=1, source_target_pairs={{0,3},{1,0},{2,1},{3,2},{4,7},{5,4},{6,5},{7,6},{8,11},{9,8},{10,9... | collective-permute-start | bytes 1081352 | tf_op jit(solution)/shard_map/ppermute | solution.py:397
  139.0 12.1 %collective-permute-start.38 = (f32[352,256]{1,0:T(8,128)S(1)}, f32[352,256]{1,0:T(8,128)S(1)}, u32[]{:S(2)}, u32[]{:S(2)}) collective-permute-start(f32[352,256]{1,0:T(8,128)S(1)} %get-tuple-element.204), channel_id=1, source_target_pairs={{0,1},{1,2},{2,3},{3,0},{4,5},{5,6},{6,7},{7,4},{8,9},{9,10},{10,1... | collective-permute-start | bytes 1081352 | tf_op jit(solution)/shard_map/ppermute | solution.py:397
  139.1 12.0 %collective-permute-start.39 = (f32[352,256]{1,0:T(8,128)S(1)}, f32[352,256]{1,0:T(8,128)S(1)}, u32[]{:S(2)}, u32[]{:S(2)}) collective-permute-start(f32[352,256]{1,0:T(8,128)S(1)} %get-tuple-element.205), channel_id=1, source_target_pairs={{0,3},{1,0},{2,1},{3,2},{4,7},{5,4},{6,5},{7,6},{8,11},{9,8},{10,9... | collective-permute-start | bytes 1081352 | tf_op jit(solution)/shard_map/ppermute | solution.py:397
  146.4 12.3 %collective-permute-start.36 = (f32[352,256]{1,0:T(8,128)S(1)}, f32[352,256]{1,0:T(8,128)S(1)}, u32[]{:S(2)}, u32[]{:S(2)}) collective-permute-start(f32[352,256]{1,0:T(8,128)S(1)} %get-tuple-element.202), channel_id=1, source_target_pairs={{0,1},{1,2},{2,3},{3,0},{4,5},{5,6},{6,7},{7,4},{8,9},{9,10},{10,1... | collective-permute-start | bytes 1081352 | tf_op jit(solution)/shard_map/ppermute | solution.py:397
  146.5 12.3 %collective-permute-start.37 = (f32[352,256]{1,0:T(8,128)S(1)}, f32[352,256]{1,0:T(8,128)S(1)}, u32[]{:S(2)}, u32[]{:S(2)}) collective-permute-start(f32[352,256]{1,0:T(8,128)S(1)} %get-tuple-element.203), channel_id=1, source_target_pairs={{0,3},{1,0},{2,1},{3,2},{4,7},{5,4},{6,5},{7,6},{8,11},{9,8},{10,9... | collective-permute-start | bytes 1081352 | tf_op jit(solution)/shard_map/ppermute | solution.py:397
  154.1 11.4 %collective-permute-start.42 = (f32[352,256]{1,0:T(8,128)S(1)}, f32[352,256]{1,0:T(8,128)S(1)}, u32[]{:S(2)}, u32[]{:S(2)}) collective-permute-start(f32[352,256]{1,0:T(8,128)S(1)} %get-tuple-element.212), channel_id=1, source_target_pairs={{0,1},{1,2},{2,3},{3,0},{4,5},{5,6},{6,7},{7,4},{8,9},{9,10},{10,1... | collective-permute-start | bytes 1081352 | tf_op jit(solution)/shard_map/ppermute | solution.py:397
  154.2 22.6 %collective-permute-start.49 = (f32[704,256]{1,0:T(8,128)S(1)}, f32[704,256]{1,0:T(8,128)S(1)}, u32[]{:S(2)}, u32[]{:S(2)}) collective-permute-start(f32[704,256]{1,0:T(8,128)S(1)} %get-tuple-element.223), channel_id=1, source_target_pairs={{0,4},{1,5},{2,6},{3,7},{4,0},{5,1},{6,2},{7,3},{8,12},{9,13},{10,... | collective-permute-start | bytes 2162696 | tf_op jit(solution)/shard_map/ppermute | solution.py:399
  156.2 10.3 %collective-permute-start.43 = (f32[352,256]{1,0:T(8,128)S(1)}, f32[352,256]{1,0:T(8,128)S(1)}, u32[]{:S(2)}, u32[]{:S(2)}) collective-permute-start(f32[352,256]{1,0:T(8,128)S(1)} %get-tuple-element.213), channel_id=1, source_target_pairs={{0,3},{1,0},{2,1},{3,2},{4,7},{5,4},{6,5},{7,6},{8,11},{9,8},{10,9... | collective-permute-start | bytes 1081352 | tf_op jit(solution)/shard_map/ppermute | solution.py:397
  161.8 11.7 %collective-permute-start.40 = (f32[352,256]{1,0:T(8,128)S(1)}, f32[352,256]{1,0:T(8,128)S(1)}, u32[]{:S(2)}, u32[]{:S(2)}) collective-permute-start(f32[352,256]{1,0:T(8,128)S(1)} %get-tuple-element.210), channel_id=1, source_target_pairs={{0,1},{1,2},{2,3},{3,0},{4,5},{5,6},{6,7},{7,4},{8,9},{9,10},{10,1... | collective-permute-start | bytes 1081352 | tf_op jit(solution)/shard_map/ppermute | solution.py:397
  161.9 11.6 %collective-permute-start.41 = (f32[352,256]{1,0:T(8,128)S(1)}, f32[352,256]{1,0:T(8,128)S(1)}, u32[]{:S(2)}, u32[]{:S(2)}) collective-permute-start(f32[352,256]{1,0:T(8,128)S(1)} %get-tuple-element.211), channel_id=1, source_target_pairs={{0,3},{1,0},{2,1},{3,2},{4,7},{5,4},{6,5},{7,6},{8,11},{9,8},{10,9... | collective-permute-start | bytes 1081352 | tf_op jit(solution)/shard_map/ppermute | solution.py:397
  165.5 25.2 %collective-permute-start.46 = (f32[704,256]{1,0:T(8,128)S(1)}, f32[704,256]{1,0:T(8,128)S(1)}, u32[]{:S(2)}, u32[]{:S(2)}) collective-permute-start(f32[704,256]{1,0:T(8,128)S(1)} %get-tuple-element.220), channel_id=1, source_target_pairs={{0,4},{1,5},{2,6},{3,7},{4,0},{5,1},{6,2},{7,3},{8,12},{9,13},{10,... | collective-permute-start | bytes 2162696 | tf_op jit(solution)/shard_map/ppermute | solution.py:399
  169.5 18.3 %collective-permute-start.47 = (f32[352,256]{1,0:T(8,128)S(1)}, f32[352,256]{1,0:T(8,128)S(1)}, u32[]{:S(2)}, u32[]{:S(2)}) collective-permute-start(f32[352,256]{1,0:T(8,128)S(1)} %get-tuple-element.221), channel_id=1, source_target_pairs={{0,1},{1,2},{2,3},{3,0},{4,5},{5,6},{6,7},{7,4},{8,9},{9,10},{10,1... | collective-permute-start | bytes 1081352 | tf_op jit(solution)/shard_map/ppermute | solution.py:397
  173.5 14.3 %collective-permute-start.48 = (f32[352,256]{1,0:T(8,128)S(1)}, f32[352,256]{1,0:T(8,128)S(1)}, u32[]{:S(2)}, u32[]{:S(2)}) collective-permute-start(f32[352,256]{1,0:T(8,128)S(1)} %get-tuple-element.222), channel_id=1, source_target_pairs={{0,3},{1,0},{2,1},{3,2},{4,7},{5,4},{6,5},{7,6},{8,11},{9,8},{10,9... | collective-permute-start | bytes 1081352 | tf_op jit(solution)/shard_map/ppermute | solution.py:397
  176.4 14.4 %collective-permute-start.44 = (f32[352,256]{1,0:T(8,128)S(1)}, f32[352,256]{1,0:T(8,128)S(1)}, u32[]{:S(2)}, u32[]{:S(2)}) collective-permute-start(f32[352,256]{1,0:T(8,128)S(1)} %get-tuple-element.218), channel_id=1, source_target_pairs={{0,1},{1,2},{2,3},{3,0},{4,5},{5,6},{6,7},{7,4},{8,9},{9,10},{10,1... | collective-permute-start | bytes 1081352 | tf_op jit(solution)/shard_map/ppermute | solution.py:397
  176.8 18.5 %collective-permute-start.45 = (f32[352,256]{1,0:T(8,128)S(1)}, f32[352,256]{1,0:T(8,128)S(1)}, u32[]{:S(2)}, u32[]{:S(2)}) collective-permute-start(f32[352,256]{1,0:T(8,128)S(1)} %get-tuple-element.219), channel_id=1, source_target_pairs={{0,3},{1,0},{2,1},{3,2},{4,7},{5,4},{6,5},{7,6},{8,11},{9,8},{10,9... | collective-permute-start | bytes 1081352 | tf_op jit(solution)/shard_map/ppermute | solution.py:397
  198.4 80.7 %all-to-all-start.1 = ((f32[16,8,8192]{2,1,0:T(8,128)}), f32[16,8,8192]{2,1,0:T(8,128)}, u32[]{:S(2)}, u32[]{:S(2)}) async-start(f32[16,8,8192]{2,1,0:T(8,128)} %get-tuple-element.228), calls=%async_computation.1 | async-start | bytes 8388608 | tf_op jit(solution)/shard_map/all_to_all | solution.py:407
  213.4 11.1 %collective-permute-start.52 = (f32[352,256]{1,0:T(8,128)S(1)}, f32[352,256]{1,0:T(8,128)S(1)}, u32[]{:S(2)}, u32[]{:S(2)}) collective-permute-start(f32[352,256]{1,0:T(8,128)S(1)} %get-tuple-element.231), channel_id=1, source_target_pairs={{0,1},{1,2},{2,3},{3,0},{4,5},{5,6},{6,7},{7,4},{8,9},{9,10},{10,1... | collective-permute-start | bytes 1081352 | tf_op jit(solution)/shard_map/ppermute | solution.py:397
  213.4 11.1 %collective-permute-start.53 = (f32[352,256]{1,0:T(8,128)S(1)}, f32[352,256]{1,0:T(8,128)S(1)}, u32[]{:S(2)}, u32[]{:S(2)}) collective-permute-start(f32[352,256]{1,0:T(8,128)S(1)} %get-tuple-element.232), channel_id=1, source_target_pairs={{0,3},{1,0},{2,1},{3,2},{4,7},{5,4},{6,5},{7,6},{8,11},{9,8},{10,9... | collective-permute-start | bytes 1081352 | tf_op jit(solution)/shard_map/ppermute | solution.py:397
  216.1 16.2 %collective-permute-start.50 = (f32[352,256]{1,0:T(8,128)S(1)}, f32[352,256]{1,0:T(8,128)S(1)}, u32[]{:S(2)}, u32[]{:S(2)}) collective-permute-start(f32[352,256]{1,0:T(8,128)S(1)} %get-tuple-element.229), channel_id=1, source_target_pairs={{0,1},{1,2},{2,3},{3,0},{4,5},{5,6},{6,7},{7,4},{8,9},{9,10},{10,1... | collective-permute-start | bytes 1081352 | tf_op jit(solution)/shard_map/ppermute | solution.py:397
  216.1 16.2 %collective-permute-start.51 = (f32[352,256]{1,0:T(8,128)S(1)}, f32[352,256]{1,0:T(8,128)S(1)}, u32[]{:S(2)}, u32[]{:S(2)}) collective-permute-start(f32[352,256]{1,0:T(8,128)S(1)} %get-tuple-element.230), channel_id=1, source_target_pairs={{0,3},{1,0},{2,1},{3,2},{4,7},{5,4},{6,5},{7,6},{8,11},{9,8},{10,9... | collective-permute-start | bytes 1081352 | tf_op jit(solution)/shard_map/ppermute | solution.py:397
  226.2 13.8 %collective-permute-start.56 = (f32[352,256]{1,0:T(8,128)S(1)}, f32[352,256]{1,0:T(8,128)S(1)}, u32[]{:S(2)}, u32[]{:S(2)}) collective-permute-start(f32[352,256]{1,0:T(8,128)S(1)} %get-tuple-element.239), channel_id=1, source_target_pairs={{0,1},{1,2},{2,3},{3,0},{4,5},{5,6},{6,7},{7,4},{8,9},{9,10},{10,1... | collective-permute-start | bytes 1081352 | tf_op jit(solution)/shard_map/ppermute | solution.py:397
  226.9 13.1 %collective-permute-start.57 = (f32[352,256]{1,0:T(8,128)S(1)}, f32[352,256]{1,0:T(8,128)S(1)}, u32[]{:S(2)}, u32[]{:S(2)}) collective-permute-start(f32[352,256]{1,0:T(8,128)S(1)} %get-tuple-element.240), channel_id=1, source_target_pairs={{0,3},{1,0},{2,1},{3,2},{4,7},{5,4},{6,5},{7,6},{8,11},{9,8},{10,9... | collective-permute-start | bytes 1081352 | tf_op jit(solution)/shard_map/ppermute | solution.py:397
  233.9 13.8 %collective-permute-start.54 = (f32[352,256]{1,0:T(8,128)S(1)}, f32[352,256]{1,0:T(8,128)S(1)}, u32[]{:S(2)}, u32[]{:S(2)}) collective-permute-start(f32[352,256]{1,0:T(8,128)S(1)} %get-tuple-element.237), channel_id=1, source_target_pairs={{0,1},{1,2},{2,3},{3,0},{4,5},{5,6},{6,7},{7,4},{8,9},{9,10},{10,1... | collective-permute-start | bytes 1081352 | tf_op jit(solution)/shard_map/ppermute | solution.py:397
  234.6 13.1 %collective-permute-start.55 = (f32[352,256]{1,0:T(8,128)S(1)}, f32[352,256]{1,0:T(8,128)S(1)}, u32[]{:S(2)}, u32[]{:S(2)}) collective-permute-start(f32[352,256]{1,0:T(8,128)S(1)} %get-tuple-element.238), channel_id=1, source_target_pairs={{0,3},{1,0},{2,1},{3,2},{4,7},{5,4},{6,5},{7,6},{8,11},{9,8},{10,9... | collective-permute-start | bytes 1081352 | tf_op jit(solution)/shard_map/ppermute | solution.py:397
  241.6 13.8 %collective-permute-start.60 = (f32[352,256]{1,0:T(8,128)S(1)}, f32[352,256]{1,0:T(8,128)S(1)}, u32[]{:S(2)}, u32[]{:S(2)}) collective-permute-start(f32[352,256]{1,0:T(8,128)S(1)} %get-tuple-element.247), channel_id=1, source_target_pairs={{0,1},{1,2},{2,3},{3,0},{4,5},{5,6},{6,7},{7,4},{8,9},{9,10},{10,1... | collective-permute-start | bytes 1081352 | tf_op jit(solution)/shard_map/ppermute | solution.py:397
  242.3 13.1 %collective-permute-start.61 = (f32[352,256]{1,0:T(8,128)S(1)}, f32[352,256]{1,0:T(8,128)S(1)}, u32[]{:S(2)}, u32[]{:S(2)}) collective-permute-start(f32[352,256]{1,0:T(8,128)S(1)} %get-tuple-element.248), channel_id=1, source_target_pairs={{0,3},{1,0},{2,1},{3,2},{4,7},{5,4},{6,5},{7,6},{8,11},{9,8},{10,9... | collective-permute-start | bytes 1081352 | tf_op jit(solution)/shard_map/ppermute | solution.py:397
  249.4 13.8 %collective-permute-start.58 = (f32[352,256]{1,0:T(8,128)S(1)}, f32[352,256]{1,0:T(8,128)S(1)}, u32[]{:S(2)}, u32[]{:S(2)}) collective-permute-start(f32[352,256]{1,0:T(8,128)S(1)} %get-tuple-element.245), channel_id=1, source_target_pairs={{0,1},{1,2},{2,3},{3,0},{4,5},{5,6},{6,7},{7,4},{8,9},{9,10},{10,1... | collective-permute-start | bytes 1081352 | tf_op jit(solution)/shard_map/ppermute | solution.py:397
  250.0 13.1 %collective-permute-start.59 = (f32[352,256]{1,0:T(8,128)S(1)}, f32[352,256]{1,0:T(8,128)S(1)}, u32[]{:S(2)}, u32[]{:S(2)}) collective-permute-start(f32[352,256]{1,0:T(8,128)S(1)} %get-tuple-element.246), channel_id=1, source_target_pairs={{0,3},{1,0},{2,1},{3,2},{4,7},{5,4},{6,5},{7,6},{8,11},{9,8},{10,9... | collective-permute-start | bytes 1081352 | tf_op jit(solution)/shard_map/ppermute | solution.py:397
  (6 other events, 52.0 us)
